TPU v7x, 768 devices: a whole 4x8x12 slice. The times are simulated.
768 devices in a mesh: gx: 96 (over y, z), gy: 8 (over x, core).
Axes of the slice: x: 4, y: 8, z: 12, core: 2. Of those that a mesh axis runs over, the one named last changes fastest.
Arguments:
- multipoles: bfloat16 [49152, 256], P(('gx', 'gy')), may hold values from -4 to 4
- operators: bfloat16 [16, 256, 256], replicated, may hold values from -0.375 to 0.375
- pairs: int32 [3, 786432], P(None, ('gx', 'gy')), may hold values from 0 to 687, as said below
- pair_count: int32 [768], P(('gx', 'gy')), may hold values from 256 to 1024, as said below
- send_list: int32 [479232], P(('gx', 'gy')), may hold values from 0 to 63
Outputs:
- local_field: float32 [49152, 256], P(('gx', 'gy'))
Inputs may be any that keep to these rules, and one draw needn't show every extreme that they name: `pairs`: A source index below 64 is the device's own box; a larger one names slot (u - 64) % 24 of neighbour lane (u - 64) // 24, and the block in that direction lies on the grid. Targets are below 64, operators below 16. `pair_count`: some device uses all 1024 slots.
All inputs are finite; a program needn't handle non-finite values.
Results may differ from a plain program's by a relative error of at most 0.00035.
Values may be sent and summed in bfloat16 or wider, within the bound.
A program may use at most 64 MiB of HBM per device.

v0:
```python
import jax
import jax.numpy as jnp
from jax import lax
from jax.sharding import PartitionSpec as P


def passed_along(block, axis, distance):
    devices = range(lax.axis_size(axis))
    route = [(i - distance, i) for i in devices if i - distance in devices]
    return lax.ppermute(block, axis, route)


def lane_directions():
    return [
        (lane_code // 9 - 1, lane_code // 3 % 3 - 1, lane_code % 3 - 1)
        for lane_code in range(27)
        if lane_code != 13
    ]


def lane_offset(heading, row_span, block_rows):
    return heading[0] + row_span * (heading[1] + block_rows * heading[2])


def fetch_sources(outgoing, block_rows):
    directions = lane_directions()
    row_span = lax.axis_size("gy")
    surface = outgoing.shape[2]
    pieces = []
    for lane_index in range(len(directions)):
        offset = lane_offset(directions[lane_index], row_span, block_rows)
        pieces.append(passed_along(outgoing[lane_index], ("gx", "gy"), -offset))
    return jnp.stack(pieces).reshape(-1, surface)


def send_back(partial_value, block_rows):
    directions = lane_directions()
    row_span = lax.axis_size("gy")
    surface = partial_value.shape[2]
    pieces = []
    for lane_index in range(len(directions)):
        offset = lane_offset(directions[lane_index], row_span, block_rows)
        pieces.append(passed_along(partial_value[lane_index], ("gx", "gy"), offset))
    return jnp.stack(pieces).reshape(-1, surface)


def local(multipoles, operators, pairs, pair_count, send_list):
    box_count, surface = multipoles.shape
    block_rows = min(8, lax.axis_size("gx") // 2)
    lane_total = len(lane_directions())
    slot_rows = send_list.shape[0]
    slot_count = slot_rows // lane_total
    source_rows = box_count + slot_rows
    outgoing = multipoles[send_list].reshape(lane_total, slot_count, surface)
    own_terms = jnp.einsum("sp,opq->osq", multipoles, operators, preferred_element_type=jnp.float32)
    mirror_terms = jnp.einsum(
        "tp,oqp->otq", multipoles, operators, preferred_element_type=jnp.float32
    )
    ghost_rows = fetch_sources(outgoing, block_rows)
    ghost_terms = jnp.einsum(
        "sp,opq->osq", ghost_rows, operators, preferred_element_type=jnp.float32
    )
    source_terms = jnp.concatenate([own_terms, ghost_terms], axis=1).reshape(-1, surface)
    mirror_table = mirror_terms.reshape(-1, surface)
    slot_total = pairs.shape[1]
    in_use = (jnp.arange(slot_total, dtype=jnp.int32) < pair_count[0])[:, None]
    source_ids = pairs[0]
    target_ids = pairs[1]
    operator_ids = pairs[2]
    forward_rows = jnp.where(in_use, source_terms[operator_ids * source_rows + source_ids], 0.0)
    local_sum = jax.ops.segment_sum(forward_rows, target_ids, box_count)
    mirror_rows = jnp.where(in_use, mirror_table[operator_ids * box_count + target_ids], 0.0)
    mirror_sum = jax.ops.segment_sum(mirror_rows, source_ids, source_rows)
    local_sum = local_sum + mirror_sum[:box_count]
    partial_value = mirror_sum[box_count:].reshape(lane_total, slot_count, surface)
    returned = send_back(partial_value, block_rows)
    local_sum = local_sum + jax.ops.segment_sum(returned, send_list, box_count)
    return local_sum


def solution(mesh):
    return jax.shard_map(
        local,
        mesh=mesh,
        in_specs=(
            P(("gx", "gy"), None),
            P(),
            P(None, ("gx", "gy")),
            P(("gx", "gy")),
            P(("gx", "gy")),
        ),
        out_specs=P(("gx", "gy"), None),
        check_vma=False,
    )
```

profile of v0, /device:TPU:32, one launch (start us, length us, event | category | flops | bytes accessed | tf_op | source)
XLA Modules:
  0.0 496.7 jit_solution(14015197109530481708)
XLA Ops:
  5.3 15.2 %collective-permute-start.6 = (bf16[24,256]{1,0:T(8,128)(2,1)}, bf16[24,256]{1,0:T(8,128)(2,1)S(1)}, u32[]{:S(2)}, u32[]{:S(2)}) collective-permute-start(bf16[24,256]{1,0:T(8,128)(2,1)} %get-tuple-element.50), channel_id=1, source_target_pairs={{0,57},{1,58},{2,59},{3,60},{4,61},{5,62},{6,63},{7,64},{8,65},{9,... | collective-permute-start | bytes 36872 | tf_op jit(solution)/shard_map/ppermute | solution.py:10
  20.5 7.2 %collective-permute-start.5 = (bf16[24,256]{1,0:T(8,128)(2,1)S(1)}, bf16[24,256]{1,0:T(8,128)(2,1)S(1)}, u32[]{:S(2)}, u32[]{:S(2)}) collective-permute-start(bf16[24,256]{1,0:T(8,128)(2,1)S(1)} %get-tuple-element.51), channel_id=1, source_target_pairs={{63,0},{64,1},{65,2},{66,3},{67,4},{68,5},{69,6},{70,7},{71,8},{72... | collective-permute-start | bytes 36872 | tf_op jit(solution)/shard_map/ppermute | solution.py:10
  29.6 5.0 collective-permute-start.3
  43.0 13.1 %scatter_custom_fusion = f32[688,256]{1,0:T(8,128)} fusion(s32[1024]{0:T(1024)S(1)} %bitcast.141, f32[]{:T(128)} %constant.6.clone.1, pred[1024]{0:T(1024)(128)(4,1)S(1)} %iota_compare_fusion, f32[1024,256]{1,0:T(8,128)} %bitcast.136, s32[1024]{0:T(1024)S(1)} %get-tuple-element.62), kind=kCustom, calls=%fused_computation.11 | custom fusion | flops 524288 | bytes 1759232 | tf_op jit(solution)/shard_map/scatter-add | solution.py:73
  59.9 3.8 collective-permute-start.1
  63.7 7.8 %collective-permute-done.1 = bf16[24,256]{1,0:T(8,128)(2,1)S(1)} collective-permute-done((bf16[24,256]{1,0:T(8,128)(2,1)}, bf16[24,256]{1,0:T(8,128)(2,1)S(1)}, u32[]{:S(2)}, u32[]{:S(2)}) %collective-permute-start.1) | collective-permute-done | bytes 12320 | tf_op jit(solution)/shard_map/ppermute | solution.py:10
  71.5 3.7 collective-permute-start.2
  75.1 10.0 %collective-permute-done.2 = bf16[24,256]{1,0:T(8,128)(2,1)S(1)} collective-permute-done((bf16[24,256]{1,0:T(8,128)(2,1)}, bf16[24,256]{1,0:T(8,128)(2,1)S(1)}, u32[]{:S(2)}, u32[]{:S(2)}) %collective-permute-start.2) | collective-permute-done | bytes 12320 | tf_op jit(solution)/shard_map/ppermute | solution.py:10
  87.0 3.5 collective-permute-start.24
  90.6 5.1 %collective-permute-start.23 = (bf16[24,256]{1,0:T(8,128)(2,1)S(1)}, bf16[24,256]{1,0:T(8,128)(2,1)S(1)}, u32[]{:S(2)}, u32[]{:S(2)}) collective-permute-start(bf16[24,256]{1,0:T(8,128)(2,1)S(1)} %get-tuple-element.33), channel_id=1, source_target_pairs={{0,55},{1,56},{2,57},{3,58},{4,59},{5,60},{6,61},{7,62},{8,63},{9,... | collective-permute-start | bytes 36872 | tf_op jit(solution)/shard_map/ppermute | solution.py:10
  95.7 5.1 %collective-permute-start.22 = (bf16[24,256]{1,0:T(8,128)(2,1)S(1)}, bf16[24,256]{1,0:T(8,128)(2,1)S(1)}, u32[]{:S(2)}, u32[]{:S(2)}) collective-permute-start(bf16[24,256]{1,0:T(8,128)(2,1)S(1)} %get-tuple-element.34), channel_id=1, source_target_pairs={{65,0},{66,1},{67,2},{68,3},{69,4},{70,5},{71,6},{72,7},{73,8},{74... | collective-permute-start | bytes 36872 | tf_op jit(solution)/shard_map/ppermute | solution.py:10
  100.9 5.8 %collective-permute-start.7 = (bf16[24,256]{1,0:T(8,128)(2,1)}, bf16[24,256]{1,0:T(8,128)(2,1)S(1)}, u32[]{:S(2)}, u32[]{:S(2)}) collective-permute-start(bf16[24,256]{1,0:T(8,128)(2,1)} %get-tuple-element.49), channel_id=1, source_target_pairs={{7,0},{8,1},{9,2},{10,3},{11,4},{12,5},{13,6},{14,7},{15,8},{16,9}... | collective-permute-start | bytes 36872 | tf_op jit(solution)/shard_map/ppermute | solution.py:10
  111.0 8.5 %collective-permute-done.8 = bf16[24,256]{1,0:T(8,128)(2,1)S(1)} collective-permute-done((bf16[24,256]{1,0:T(8,128)(2,1)}, bf16[24,256]{1,0:T(8,128)(2,1)S(1)}, u32[]{:S(2)}, u32[]{:S(2)}) %collective-permute-start.8) | collective-permute-done | bytes 12320 | tf_op jit(solution)/shard_map/ppermute | solution.py:10
  122.4 6.8 %collective-permute-done.9 = bf16[24,256]{1,0:T(8,128)(2,1)S(1)} collective-permute-done((bf16[24,256]{1,0:T(8,128)(2,1)}, bf16[24,256]{1,0:T(8,128)(2,1)S(1)}, u32[]{:S(2)}, u32[]{:S(2)}) %collective-permute-start.9) | collective-permute-done | bytes 12320 | tf_op jit(solution)/shard_map/ppermute | solution.py:10
  129.2 3.1 collective-permute-start.10
  132.3 6.0 %collective-permute-done.10 = bf16[24,256]{1,0:T(8,128)(2,1)S(1)} collective-permute-done((bf16[24,256]{1,0:T(8,128)(2,1)}, bf16[24,256]{1,0:T(8,128)(2,1)S(1)}, u32[]{:S(2)}, u32[]{:S(2)}) %collective-permute-start.10) | collective-permute-done | bytes 12320 | tf_op jit(solution)/shard_map/ppermute | solution.py:10
  138.3 6.2 %collective-permute-start.11 = (bf16[24,256]{1,0:T(8,128)(2,1)}, bf16[24,256]{1,0:T(8,128)(2,1)S(1)}, u32[]{:S(2)}, u32[]{:S(2)}) collective-permute-start(bf16[24,256]{1,0:T(8,128)(2,1)} %get-tuple-element.45), channel_id=1, source_target_pairs={{56,0},{57,1},{58,2},{59,3},{60,4},{61,5},{62,6},{63,7},{64,8},{65... | collective-permute-start | bytes 36872 | tf_op jit(solution)/shard_map/ppermute | solution.py:10
  144.5 5.6 %collective-permute-done.11 = bf16[24,256]{1,0:T(8,128)(2,1)S(1)} collective-permute-done((bf16[24,256]{1,0:T(8,128)(2,1)}, bf16[24,256]{1,0:T(8,128)(2,1)S(1)}, u32[]{:S(2)}, u32[]{:S(2)}) %collective-permute-start.11) | collective-permute-done | bytes 12320 | tf_op jit(solution)/shard_map/ppermute | solution.py:10
  150.1 7.7 %collective-permute-start.12 = (bf16[24,256]{1,0:T(8,128)(2,1)}, bf16[24,256]{1,0:T(8,128)(2,1)S(1)}, u32[]{:S(2)}, u32[]{:S(2)}) collective-permute-start(bf16[24,256]{1,0:T(8,128)(2,1)} %get-tuple-element.44), channel_id=1, source_target_pairs={{0,64},{1,65},{2,66},{3,67},{4,68},{5,69},{6,70},{7,71},{8,72},{9,... | collective-permute-start | bytes 36872 | tf_op jit(solution)/shard_map/ppermute | solution.py:10
  157.8 4.1 collective-permute-done.12
  161.9 3.2 collective-permute-start.13
  165.1 6.5 %collective-permute-done.13 = bf16[24,256]{1,0:T(8,128)(2,1)S(1)} collective-permute-done((bf16[24,256]{1,0:T(8,128)(2,1)}, bf16[24,256]{1,0:T(8,128)(2,1)S(1)}, u32[]{:S(2)}, u32[]{:S(2)}) %collective-permute-start.13) | collective-permute-done | bytes 12320 | tf_op jit(solution)/shard_map/ppermute | solution.py:10
  171.6 8.7 %collective-permute-start.14 = (bf16[24,256]{1,0:T(8,128)(2,1)}, bf16[24,256]{1,0:T(8,128)(2,1)S(1)}, u32[]{:S(2)}, u32[]{:S(2)}) collective-permute-start(bf16[24,256]{1,0:T(8,128)(2,1)} %get-tuple-element.42), channel_id=1, source_target_pairs={{0,56},{1,57},{2,58},{3,59},{4,60},{5,61},{6,62},{7,63},{8,64},{9,... | collective-permute-start | bytes 36872 | tf_op jit(solution)/shard_map/ppermute | solution.py:10
  180.4 3.9 collective-permute-done.14
  184.3 3.8 collective-permute-start.15
  192.8 6.1 %collective-permute-done.16 = bf16[24,256]{1,0:T(8,128)(2,1)S(1)} collective-permute-done((bf16[24,256]{1,0:T(8,128)(2,1)}, bf16[24,256]{1,0:T(8,128)(2,1)S(1)}, u32[]{:S(2)}, u32[]{:S(2)}) %collective-permute-start.16) | collective-permute-done | bytes 12320 | tf_op jit(solution)/shard_map/ppermute | solution.py:10
  200.8 7.2 %collective-permute-done.17 = bf16[24,256]{1,0:T(8,128)(2,1)S(1)} collective-permute-done((bf16[24,256]{1,0:T(8,128)(2,1)}, bf16[24,256]{1,0:T(8,128)(2,1)S(1)}, u32[]{:S(2)}, u32[]{:S(2)}) %collective-permute-start.17) | collective-permute-done | bytes 12320 | tf_op jit(solution)/shard_map/ppermute | solution.py:10
  208.0 4.3 collective-permute-start.18
  212.3 4.0 collective-permute-done.18
  216.3 3.6 collective-permute-start.19
  220.0 7.4 %collective-permute-done.19 = bf16[24,256]{1,0:T(8,128)(2,1)S(1)} collective-permute-done((bf16[24,256]{1,0:T(8,128)(2,1)S(1)}, bf16[24,256]{1,0:T(8,128)(2,1)S(1)}, u32[]{:S(2)}, u32[]{:S(2)}) %collective-permute-start.19) | collective-permute-done | bytes 12320 | tf_op jit(solution)/shard_map/ppermute | solution.py:10
  227.4 8.3 %collective-permute-start.20 = (bf16[24,256]{1,0:T(8,128)(2,1)S(1)}, bf16[24,256]{1,0:T(8,128)(2,1)S(1)}, u32[]{:S(2)}, u32[]{:S(2)}) collective-permute-start(bf16[24,256]{1,0:T(8,128)(2,1)S(1)} %get-tuple-element.36), channel_id=1, source_target_pairs={{0,63},{1,64},{2,65},{3,66},{4,67},{5,68},{6,69},{7,70},{8,71},{9,... | collective-permute-start | bytes 36872 | tf_op jit(solution)/shard_map/ppermute | solution.py:10
  238.4 8.7 %collective-permute-start.21 = (bf16[24,256]{1,0:T(8,128)(2,1)S(1)}, bf16[24,256]{1,0:T(8,128)(2,1)S(1)}, u32[]{:S(2)}, u32[]{:S(2)}) collective-permute-start(bf16[24,256]{1,0:T(8,128)(2,1)S(1)} %get-tuple-element.35), channel_id=1, source_target_pairs={{1,0},{2,1},{3,2},{4,3},{5,4},{6,5},{7,6},{8,7},{9,8},{10,9},{11,1... | collective-permute-start | bytes 36872 | tf_op jit(solution)/shard_map/ppermute | solution.py:10
  248.4 4.6 collective-permute-start.32
  253.1 6.0 %collective-permute-start.31 = (f32[24,256]{1,0:T(8,128)}, f32[24,256]{1,0:T(8,128)S(1)}, u32[]{:S(2)}, u32[]{:S(2)}) collective-permute-start(f32[24,256]{1,0:T(8,128)} %get-tuple-element.25), channel_id=1, source_target_pairs={{0,63},{1,64},{2,65},{3,66},{4,67},{5,68},{6,69},{7,70},{8,71},{9,... | collective-permute-start | bytes 73736 | tf_op jit(solution)/shard_map/ppermute | solution.py:10
  265.8 5.3 %convolution_bitcast_fusion = f32[16,624,256]{2,1,0:T(8,128)} fusion(bf16[624,256,1]{1,0,2:T(8,128)(2,1)S(1)} %bitcast.137, bf16[16,256,256]{2,1,0:T(8,128)(2,1)S(1)} %copy-done), kind=kOutput, calls=%fused_computation.7 | convolution fusion | flops 1308622848 | bytes 12640256 | tf_op jit(solution)/shard_map/sp,opq->osq/dot_general | solution.py:60
  271.1 9.0 %pad_maximum_fusion = f32[16,688,256]{2,1,0:T(8,128)} fusion(f32[16,624,256]{2,1,0:T(8,128)} %convolution_bitcast_fusion, f32[16,64,256]{2,1,0:T(8,128)S(1)} %convolution_bitcast_fusion.1), kind=kLoop, calls=%fused_computation.6 | loop fusion | flops 2818048 | bytes 22544384 | tf_op jit(solution)/shard_map/concatenate | solution.py:63
  280.2 13.1 %scatter_custom_fusion.1 = f32[64,256]{1,0:T(8,128)S(1)} fusion(f32[64,256]{1,0:T(8,128)S(1)} %slice-done, s32[1024]{0:T(1024)} %bitcast.140, f32[]{:T(128)} %constant.6.clone.1, pred[1024]{0:T(1024)(128)(4,1)} %copy-done.13, f32[11008,256]{1,0:T(8,128)} %bitcast.135, s32[1024]{0:T(1024)} %broadcast_clamp_fusion), kind=kCustom, calls=%fused_computation.9 | custom fusion | flops 524288 | bytes 11343360 | tf_op jit(solution)/shard_map/scatter-add | solution.py:71
  295.3 6.7 %collective-permute-done.27 = f32[24,256]{1,0:T(8,128)S(1)} collective-permute-done((f32[24,256]{1,0:T(8,128)S(1)}, f32[24,256]{1,0:T(8,128)S(1)}, u32[]{:S(2)}, u32[]{:S(2)}) %collective-permute-start.27) | collective-permute-done | bytes 24608 | tf_op jit(solution)/shard_map/ppermute | solution.py:10
  301.9 7.8 %collective-permute-start.28 = (f32[24,256]{1,0:T(8,128)S(1)}, f32[24,256]{1,0:T(8,128)S(1)}, u32[]{:S(2)}, u32[]{:S(2)}) collective-permute-start(f32[24,256]{1,0:T(8,128)S(1)} %copy-done.11), channel_id=1, source_target_pairs={{0,55},{1,56},{2,57},{3,58},{4,59},{5,60},{6,61},{7,62},{8,63},{9,... | collective-permute-start | bytes 73736 | tf_op jit(solution)/shard_map/ppermute | solution.py:10
  309.8 4.2 collective-permute-done.28
  314.0 3.7 collective-permute-start.51
  317.7 4.3 collective-permute-start.50
  322.0 14.5 %collective-permute-start.49 = (f32[24,256]{1,0:T(8,128)S(1)}, f32[24,256]{1,0:T(8,128)S(1)}, u32[]{:S(2)}, u32[]{:S(2)}) collective-permute-start(f32[24,256]{1,0:T(8,128)S(1)} %get-tuple-element.7), channel_id=1, source_target_pairs={{55,0},{56,1},{57,2},{58,3},{59,4},{60,5},{61,6},{62,7},{63,8},{64... | collective-permute-start | bytes 73736 | tf_op jit(solution)/shard_map/ppermute | solution.py:10
  341.7 5.4 %collective-permute-done.33 = f32[24,256]{1,0:T(8,128)S(1)} collective-permute-done((f32[24,256]{1,0:T(8,128)S(1)}, f32[24,256]{1,0:T(8,128)S(1)}, u32[]{:S(2)}, u32[]{:S(2)}) %collective-permute-start.33) | collective-permute-done | bytes 24608 | tf_op jit(solution)/shard_map/ppermute | solution.py:10
  349.0 7.1 %collective-permute-done.34 = f32[24,256]{1,0:T(8,128)S(1)} collective-permute-done((f32[24,256]{1,0:T(8,128)S(1)}, f32[24,256]{1,0:T(8,128)S(1)}, u32[]{:S(2)}, u32[]{:S(2)}) %collective-permute-start.34) | collective-permute-done | bytes 24608 | tf_op jit(solution)/shard_map/ppermute | solution.py:10
  356.1 5.2 %collective-permute-start.35 = (f32[24,256]{1,0:T(8,128)S(1)}, f32[24,256]{1,0:T(8,128)S(1)}, u32[]{:S(2)}, u32[]{:S(2)}) collective-permute-start(f32[24,256]{1,0:T(8,128)S(1)} %copy-done.8), channel_id=1, source_target_pairs={{72,0},{73,1},{74,2},{75,3},{76,4},{77,5},{78,6},{79,7},{80,8},{81... | collective-permute-start | bytes 73736 | tf_op jit(solution)/shard_map/ppermute | solution.py:10
  361.3 4.1 collective-permute-done.35
  367.3 3.8 collective-permute-done.36
  371.0 5.7 %collective-permute-start.37 = (f32[24,256]{1,0:T(8,128)S(1)}, f32[24,256]{1,0:T(8,128)S(1)}, u32[]{:S(2)}, u32[]{:S(2)}) collective-permute-start(f32[24,256]{1,0:T(8,128)S(1)} %copy-done.6), channel_id=1, source_target_pairs={{0,56},{1,57},{2,58},{3,59},{4,60},{5,61},{6,62},{7,63},{8,64},{9,... | collective-permute-start | bytes 73736 | tf_op jit(solution)/shard_map/ppermute | solution.py:10
  376.8 7.2 %collective-permute-done.37 = f32[24,256]{1,0:T(8,128)S(1)} collective-permute-done((f32[24,256]{1,0:T(8,128)S(1)}, f32[24,256]{1,0:T(8,128)S(1)}, u32[]{:S(2)}, u32[]{:S(2)}) %collective-permute-start.37) | collective-permute-done | bytes 24608 | tf_op jit(solution)/shard_map/ppermute | solution.py:10
  384.0 4.9 collective-permute-start.38
  388.9 4.7 collective-permute-done.38
  395.5 9.8 %collective-permute-done.39 = f32[24,256]{1,0:T(8,128)S(1)} collective-permute-done((f32[24,256]{1,0:T(8,128)S(1)}, f32[24,256]{1,0:T(8,128)S(1)}, u32[]{:S(2)}, u32[]{:S(2)}) %collective-permute-start.39) | collective-permute-done | bytes 24608 | tf_op jit(solution)/shard_map/ppermute | solution.py:10
  405.3 7.4 %collective-permute-start.40 = (f32[24,256]{1,0:T(8,128)S(1)}, f32[24,256]{1,0:T(8,128)S(1)}, u32[]{:S(2)}, u32[]{:S(2)}) collective-permute-start(f32[24,256]{1,0:T(8,128)S(1)} %copy-done.3), channel_id=1, source_target_pairs={{56,0},{57,1},{58,2},{59,3},{60,4},{61,5},{62,6},{63,7},{64,8},{65... | collective-permute-start | bytes 73736 | tf_op jit(solution)/shard_map/ppermute | solution.py:10
  412.7 4.3 collective-permute-done.40
  419.0 7.1 %collective-permute-done.41 = f32[24,256]{1,0:T(8,128)S(1)} collective-permute-done((f32[24,256]{1,0:T(8,128)S(1)}, f32[24,256]{1,0:T(8,128)S(1)}, u32[]{:S(2)}, u32[]{:S(2)}) %collective-permute-start.41) | collective-permute-done | bytes 24608 | tf_op jit(solution)/shard_map/ppermute | solution.py:10
  428.0 7.7 %collective-permute-done.42 = f32[24,256]{1,0:T(8,128)S(1)} collective-permute-done((f32[24,256]{1,0:T(8,128)S(1)}, f32[24,256]{1,0:T(8,128)S(1)}, u32[]{:S(2)}, u32[]{:S(2)}) %collective-permute-start.42) | collective-permute-done | bytes 24608 | tf_op jit(solution)/shard_map/ppermute | solution.py:10
  437.6 9.2 %collective-permute-done.43 = f32[24,256]{1,0:T(8,128)S(1)} collective-permute-done((f32[24,256]{1,0:T(8,128)S(1)}, f32[24,256]{1,0:T(8,128)S(1)}, u32[]{:S(2)}, u32[]{:S(2)}) %collective-permute-start.43) | collective-permute-done | bytes 24608 | tf_op jit(solution)/shard_map/ppermute | solution.py:10
  448.8 4.4 collective-permute-done.44
  455.4 11.1 %collective-permute-done.45 = f32[24,256]{1,0:T(8,128)S(1)} collective-permute-done((f32[24,256]{1,0:T(8,128)S(1)}, f32[24,256]{1,0:T(8,128)S(1)}, u32[]{:S(2)}, u32[]{:S(2)}) %collective-permute-start.45) | collective-permute-done | bytes 24608 | tf_op jit(solution)/shard_map/ppermute | solution.py:10
  469.0 10.7 %collective-permute-done.46 = f32[24,256]{1,0:T(8,128)S(1)} collective-permute-done((f32[24,256]{1,0:T(8,128)S(1)}, f32[24,256]{1,0:T(8,128)S(1)}, u32[]{:S(2)}, u32[]{:S(2)}) %collective-permute-start.46) | collective-permute-done | bytes 24608 | tf_op jit(solution)/shard_map/ppermute | solution.py:10
  481.6 8.6 %collective-permute-done.47 = f32[24,256]{1,0:T(8,128)S(1)} collective-permute-done((f32[24,256]{1,0:T(8,128)S(1)}, f32[24,256]{1,0:T(8,128)S(1)}, u32[]{:S(2)}, u32[]{:S(2)}) %collective-permute-start.47) | collective-permute-done | bytes 24608 | tf_op jit(solution)/shard_map/ppermute | solution.py:10
  490.4 5.7 %scatter_custom_fusion.2 = f32[64,256]{1,0:T(8,128)S(1)} fusion(s32[624]{0:T(1024)} %param.9, f32[624,256]{1,0:T(8,128)S(1)} %bitcast.142, f32[]{:T(128)} %constant.6.clone.1), kind=kCustom, calls=%fused_computation.73 | custom fusion | flops 159744 | bytes 66048 | tf_op jit(solution)/shard_map/scatter-add | solution.py:77
  (141 shorter events, 72.9 us)
Async XLA Ops:
  0.0 38.6 %copy-start = (bf16[16,256,256]{2,1,0:T(8,128)(2,1)S(1)}, bf16[16,256,256]{2,1,0:T(8,128)(2,1)}, u32[]{:S(2)}) copy-start(bf16[16,256,256]{2,1,0:T(8,128)(2,1)} %param.6) | copy-start | bytes 6291460
  5.3 95.6 %collective-permute-start.6 = (bf16[24,256]{1,0:T(8,128)(2,1)}, bf16[24,256]{1,0:T(8,128)(2,1)S(1)}, u32[]{:S(2)}, u32[]{:S(2)}) collective-permute-start(bf16[24,256]{1,0:T(8,128)(2,1)} %get-tuple-element.50), channel_id=1, source_target_pairs={{0,57},{1,58},{2,59},{3,60},{4,61},{5,62},{6,63},{7,64},{8,65},{9,... | collective-permute-start | bytes 36872 | tf_op jit(solution)/shard_map/ppermute | solution.py:10
  20.5 75.2 %collective-permute-start.5 = (bf16[24,256]{1,0:T(8,128)(2,1)S(1)}, bf16[24,256]{1,0:T(8,128)(2,1)S(1)}, u32[]{:S(2)}, u32[]{:S(2)}) collective-permute-start(bf16[24,256]{1,0:T(8,128)(2,1)S(1)} %get-tuple-element.51), channel_id=1, source_target_pairs={{63,0},{64,1},{65,2},{66,3},{67,4},{68,5},{69,6},{70,7},{71,8},{72... | collective-permute-start | bytes 36872 | tf_op jit(solution)/shard_map/ppermute | solution.py:10
  27.7 62.9 %collective-permute-start.4 = (bf16[24,256]{1,0:T(8,128)(2,1)}, bf16[24,256]{1,0:T(8,128)(2,1)S(1)}, u32[]{:S(2)}, u32[]{:S(2)}) collective-permute-start(bf16[24,256]{1,0:T(8,128)(2,1)} %get-tuple-element.52), channel_id=1, source_target_pairs={{0,1},{1,2},{2,3},{3,4},{4,5},{5,6},{6,7},{7,8},{8,9},{9,10},{10,1... | collective-permute-start | bytes 36872 | tf_op jit(solution)/shard_map/ppermute | solution.py:10
  29.6 57.4 %collective-permute-start.3 = (bf16[24,256]{1,0:T(8,128)(2,1)}, bf16[24,256]{1,0:T(8,128)(2,1)S(1)}, u32[]{:S(2)}, u32[]{:S(2)}) collective-permute-start(bf16[24,256]{1,0:T(8,128)(2,1)} %get-tuple-element.53), channel_id=1, source_target_pairs={{0,65},{1,66},{2,67},{3,68},{4,69},{5,70},{6,71},{7,72},{8,73},{9,... | collective-permute-start | bytes 36872 | tf_op jit(solution)/shard_map/ppermute | solution.py:10
  34.6 25.3 %collective-permute-start = (bf16[24,256]{1,0:T(8,128)(2,1)}, bf16[24,256]{1,0:T(8,128)(2,1)S(1)}, u32[]{:S(2)}, u32[]{:S(2)}) collective-permute-start(bf16[24,256]{1,0:T(8,128)(2,1)} %get-tuple-element.56), channel_id=1, source_target_pairs={{0,73},{1,74},{2,75},{3,76},{4,77},{5,78},{6,79},{7,80},{8,81},{9,... | collective-permute-start | bytes 36872 | tf_op jit(solution)/shard_map/ppermute | solution.py:10
  59.9 11.5 %collective-permute-start.1 = (bf16[24,256]{1,0:T(8,128)(2,1)}, bf16[24,256]{1,0:T(8,128)(2,1)S(1)}, u32[]{:S(2)}, u32[]{:S(2)}) collective-permute-start(bf16[24,256]{1,0:T(8,128)(2,1)} %get-tuple-element.55), channel_id=1, source_target_pairs={{0,9},{1,10},{2,11},{3,12},{4,13},{5,14},{6,15},{7,16},{8,17},{9,1... | collective-permute-start | bytes 36872 | tf_op jit(solution)/shard_map/ppermute | solution.py:10
  71.5 13.6 %collective-permute-start.2 = (bf16[24,256]{1,0:T(8,128)(2,1)}, bf16[24,256]{1,0:T(8,128)(2,1)S(1)}, u32[]{:S(2)}, u32[]{:S(2)}) collective-permute-start(bf16[24,256]{1,0:T(8,128)(2,1)} %get-tuple-element.54), channel_id=1, source_target_pairs={{55,0},{56,1},{57,2},{58,3},{59,4},{60,5},{61,6},{62,7},{63,8},{64... | collective-permute-start | bytes 36872 | tf_op jit(solution)/shard_map/ppermute | solution.py:10
  85.1 178.7 %collective-permute-start.25 = (bf16[24,256]{1,0:T(8,128)(2,1)S(1)}, bf16[24,256]{1,0:T(8,128)(2,1)S(1)}, u32[]{:S(2)}, u32[]{:S(2)}) collective-permute-start(bf16[24,256]{1,0:T(8,128)(2,1)S(1)} %get-tuple-element.31), channel_id=1, source_target_pairs={{73,0},{74,1},{75,2},{76,3},{77,4},{78,5},{79,6},{80,7},{81,8},{82... | collective-permute-start | bytes 36872 | tf_op jit(solution)/shard_map/ppermute | solution.py:10
  87.0 174.8 %collective-permute-start.24 = (bf16[24,256]{1,0:T(8,128)(2,1)S(1)}, bf16[24,256]{1,0:T(8,128)(2,1)S(1)}, u32[]{:S(2)}, u32[]{:S(2)}) collective-permute-start(bf16[24,256]{1,0:T(8,128)(2,1)S(1)} %get-tuple-element.32), channel_id=1, source_target_pairs={{9,0},{10,1},{11,2},{12,3},{13,4},{14,5},{15,6},{16,7},{17,8},{18,... | collective-permute-start | bytes 36872 | tf_op jit(solution)/shard_map/ppermute | solution.py:10
  90.6 168.6 %collective-permute-start.23 = (bf16[24,256]{1,0:T(8,128)(2,1)S(1)}, bf16[24,256]{1,0:T(8,128)(2,1)S(1)}, u32[]{:S(2)}, u32[]{:S(2)}) collective-permute-start(bf16[24,256]{1,0:T(8,128)(2,1)S(1)} %get-tuple-element.33), channel_id=1, source_target_pairs={{0,55},{1,56},{2,57},{3,58},{4,59},{5,60},{6,61},{7,62},{8,63},{9,... | collective-permute-start | bytes 36872 | tf_op jit(solution)/shard_map/ppermute | solution.py:10
  95.7 157.3 %collective-permute-start.22 = (bf16[24,256]{1,0:T(8,128)(2,1)S(1)}, bf16[24,256]{1,0:T(8,128)(2,1)S(1)}, u32[]{:S(2)}, u32[]{:S(2)}) collective-permute-start(bf16[24,256]{1,0:T(8,128)(2,1)S(1)} %get-tuple-element.34), channel_id=1, source_target_pairs={{65,0},{66,1},{67,2},{68,3},{69,4},{70,5},{71,6},{72,7},{73,8},{74... | collective-permute-start | bytes 36872 | tf_op jit(solution)/shard_map/ppermute | solution.py:10
  100.9 7.4 %collective-permute-start.7 = (bf16[24,256]{1,0:T(8,128)(2,1)}, bf16[24,256]{1,0:T(8,128)(2,1)S(1)}, u32[]{:S(2)}, u32[]{:S(2)}) collective-permute-start(bf16[24,256]{1,0:T(8,128)(2,1)} %get-tuple-element.49), channel_id=1, source_target_pairs={{7,0},{8,1},{9,2},{10,3},{11,4},{12,5},{13,6},{14,7},{15,8},{16,9}... | collective-permute-start | bytes 36872 | tf_op jit(solution)/shard_map/ppermute | solution.py:10
  108.3 11.2 %collective-permute-start.8 = (bf16[24,256]{1,0:T(8,128)(2,1)}, bf16[24,256]{1,0:T(8,128)(2,1)S(1)}, u32[]{:S(2)}, u32[]{:S(2)}) collective-permute-start(bf16[24,256]{1,0:T(8,128)(2,1)} %get-tuple-element.48), channel_id=1, source_target_pairs={{71,0},{72,1},{73,2},{74,3},{75,4},{76,5},{77,6},{78,7},{79,8},{80... | collective-permute-start | bytes 36872 | tf_op jit(solution)/shard_map/ppermute | solution.py:10
  119.5 9.7 %collective-permute-start.9 = (bf16[24,256]{1,0:T(8,128)(2,1)}, bf16[24,256]{1,0:T(8,128)(2,1)S(1)}, u32[]{:S(2)}, u32[]{:S(2)}) collective-permute-start(bf16[24,256]{1,0:T(8,128)(2,1)} %get-tuple-element.47), channel_id=1, source_target_pairs={{0,72},{1,73},{2,74},{3,75},{4,76},{5,77},{6,78},{7,79},{8,80},{9,... | collective-permute-start | bytes 36872 | tf_op jit(solution)/shard_map/ppermute | solution.py:10
  129.2 9.1 %collective-permute-start.10 = (bf16[24,256]{1,0:T(8,128)(2,1)}, bf16[24,256]{1,0:T(8,128)(2,1)S(1)}, u32[]{:S(2)}, u32[]{:S(2)}) collective-permute-start(bf16[24,256]{1,0:T(8,128)(2,1)} %get-tuple-element.46), channel_id=1, source_target_pairs={{0,8},{1,9},{2,10},{3,11},{4,12},{5,13},{6,14},{7,15},{8,16},{9,17... | collective-permute-start | bytes 36872 | tf_op jit(solution)/shard_map/ppermute | solution.py:10
  138.3 11.8 %collective-permute-start.11 = (bf16[24,256]{1,0:T(8,128)(2,1)}, bf16[24,256]{1,0:T(8,128)(2,1)S(1)}, u32[]{:S(2)}, u32[]{:S(2)}) collective-permute-start(bf16[24,256]{1,0:T(8,128)(2,1)} %get-tuple-element.45), channel_id=1, source_target_pairs={{56,0},{57,1},{58,2},{59,3},{60,4},{61,5},{62,6},{63,7},{64,8},{65... | collective-permute-start | bytes 36872 | tf_op jit(solution)/shard_map/ppermute | solution.py:10
  150.1 11.8 %collective-permute-start.12 = (bf16[24,256]{1,0:T(8,128)(2,1)}, bf16[24,256]{1,0:T(8,128)(2,1)S(1)}, u32[]{:S(2)}, u32[]{:S(2)}) collective-permute-start(bf16[24,256]{1,0:T(8,128)(2,1)} %get-tuple-element.44), channel_id=1, source_target_pairs={{0,64},{1,65},{2,66},{3,67},{4,68},{5,69},{6,70},{7,71},{8,72},{9,... | collective-permute-start | bytes 36872 | tf_op jit(solution)/shard_map/ppermute | solution.py:10
  161.9 9.7 %collective-permute-start.13 = (bf16[24,256]{1,0:T(8,128)(2,1)}, bf16[24,256]{1,0:T(8,128)(2,1)S(1)}, u32[]{:S(2)}, u32[]{:S(2)}) collective-permute-start(bf16[24,256]{1,0:T(8,128)(2,1)} %get-tuple-element.43), channel_id=1, source_target_pairs={{64,0},{65,1},{66,2},{67,3},{68,4},{69,5},{70,6},{71,7},{72,8},{73... | collective-permute-start | bytes 36872 | tf_op jit(solution)/shard_map/ppermute | solution.py:10
  171.6 12.7 %collective-permute-start.14 = (bf16[24,256]{1,0:T(8,128)(2,1)}, bf16[24,256]{1,0:T(8,128)(2,1)S(1)}, u32[]{:S(2)}, u32[]{:S(2)}) collective-permute-start(bf16[24,256]{1,0:T(8,128)(2,1)} %get-tuple-element.42), channel_id=1, source_target_pairs={{0,56},{1,57},{2,58},{3,59},{4,60},{5,61},{6,62},{7,63},{8,64},{9,... | collective-permute-start | bytes 36872 | tf_op jit(solution)/shard_map/ppermute | solution.py:10
  184.3 5.8 %collective-permute-start.15 = (bf16[24,256]{1,0:T(8,128)(2,1)}, bf16[24,256]{1,0:T(8,128)(2,1)S(1)}, u32[]{:S(2)}, u32[]{:S(2)}) collective-permute-start(bf16[24,256]{1,0:T(8,128)(2,1)} %get-tuple-element.41), channel_id=1, source_target_pairs={{8,0},{9,1},{10,2},{11,3},{12,4},{13,5},{14,6},{15,7},{16,8},{17,9... | collective-permute-start | bytes 36872 | tf_op jit(solution)/shard_map/ppermute | solution.py:10
  190.1 8.8 %collective-permute-start.16 = (bf16[24,256]{1,0:T(8,128)(2,1)}, bf16[24,256]{1,0:T(8,128)(2,1)S(1)}, u32[]{:S(2)}, u32[]{:S(2)}) collective-permute-start(bf16[24,256]{1,0:T(8,128)(2,1)} %get-tuple-element.40), channel_id=1, source_target_pairs={{72,0},{73,1},{74,2},{75,3},{76,4},{77,5},{78,6},{79,7},{80,8},{81... | collective-permute-start | bytes 36872 | tf_op jit(solution)/shard_map/ppermute | solution.py:10
  198.9 9.1 %collective-permute-start.17 = (bf16[24,256]{1,0:T(8,128)(2,1)}, bf16[24,256]{1,0:T(8,128)(2,1)S(1)}, u32[]{:S(2)}, u32[]{:S(2)}) collective-permute-start(bf16[24,256]{1,0:T(8,128)(2,1)} %get-tuple-element.39), channel_id=1, source_target_pairs={{0,71},{1,72},{2,73},{3,74},{4,75},{5,76},{6,77},{7,78},{8,79},{9,... | collective-permute-start | bytes 36872 | tf_op jit(solution)/shard_map/ppermute | solution.py:10
  208.0 8.3 %collective-permute-start.18 = (bf16[24,256]{1,0:T(8,128)(2,1)S(1)}, bf16[24,256]{1,0:T(8,128)(2,1)S(1)}, u32[]{:S(2)}, u32[]{:S(2)}) collective-permute-start(bf16[24,256]{1,0:T(8,128)(2,1)S(1)} %get-tuple-element.38), channel_id=1, source_target_pairs={{0,7},{1,8},{2,9},{3,10},{4,11},{5,12},{6,13},{7,14},{8,15},{9,16}... | collective-permute-start | bytes 36872 | tf_op jit(solution)/shard_map/ppermute | solution.py:10
  216.3 11.0 %collective-permute-start.19 = (bf16[24,256]{1,0:T(8,128)(2,1)S(1)}, bf16[24,256]{1,0:T(8,128)(2,1)S(1)}, u32[]{:S(2)}, u32[]{:S(2)}) collective-permute-start(bf16[24,256]{1,0:T(8,128)(2,1)S(1)} %get-tuple-element.37), channel_id=1, source_target_pairs={{57,0},{58,1},{59,2},{60,3},{61,4},{62,5},{63,6},{64,7},{65,8},{66... | collective-permute-start | bytes 36872 | tf_op jit(solution)/shard_map/ppermute | solution.py:10
  227.4 11.0 %collective-permute-start.20 = (bf16[24,256]{1,0:T(8,128)(2,1)S(1)}, bf16[24,256]{1,0:T(8,128)(2,1)S(1)}, u32[]{:S(2)}, u32[]{:S(2)}) collective-permute-start(bf16[24,256]{1,0:T(8,128)(2,1)S(1)} %get-tuple-element.36), channel_id=1, source_target_pairs={{0,63},{1,64},{2,65},{3,66},{4,67},{5,68},{6,69},{7,70},{8,71},{9,... | collective-permute-start | bytes 36872 | tf_op jit(solution)/shard_map/ppermute | solution.py:10
  238.4 10.1 %collective-permute-start.21 = (bf16[24,256]{1,0:T(8,128)(2,1)S(1)}, bf16[24,256]{1,0:T(8,128)(2,1)S(1)}, u32[]{:S(2)}, u32[]{:S(2)}) collective-permute-start(bf16[24,256]{1,0:T(8,128)(2,1)S(1)} %get-tuple-element.35), channel_id=1, source_target_pairs={{1,0},{2,1},{3,2},{4,3},{5,4},{6,5},{7,6},{8,7},{9,8},{10,9},{11,1... | collective-permute-start | bytes 36872 | tf_op jit(solution)/shard_map/ppermute | solution.py:10
  248.4 90.1 %collective-permute-start.32 = (f32[24,256]{1,0:T(8,128)}, f32[24,256]{1,0:T(8,128)S(1)}, u32[]{:S(2)}, u32[]{:S(2)}) collective-permute-start(f32[24,256]{1,0:T(8,128)} %get-tuple-element.24), channel_id=1, source_target_pairs={{57,0},{58,1},{59,2},{60,3},{61,4},{62,5},{63,6},{64,7},{65,8},{66... | collective-permute-start | bytes 73736 | tf_op jit(solution)/shard_map/ppermute | solution.py:10
  253.1 83.5 %collective-permute-start.31 = (f32[24,256]{1,0:T(8,128)}, f32[24,256]{1,0:T(8,128)S(1)}, u32[]{:S(2)}, u32[]{:S(2)}) collective-permute-start(f32[24,256]{1,0:T(8,128)} %get-tuple-element.25), channel_id=1, source_target_pairs={{0,63},{1,64},{2,65},{3,66},{4,67},{5,68},{6,69},{7,70},{8,71},{9,... | collective-permute-start | bytes 73736 | tf_op jit(solution)/shard_map/ppermute | solution.py:10
  259.1 62.9 %collective-permute-start.30 = (f32[24,256]{1,0:T(8,128)}, f32[24,256]{1,0:T(8,128)S(1)}, u32[]{:S(2)}, u32[]{:S(2)}) collective-permute-start(f32[24,256]{1,0:T(8,128)} %get-tuple-element.26), channel_id=1, source_target_pairs={{1,0},{2,1},{3,2},{4,3},{5,4},{6,5},{7,6},{8,7},{9,8},{10,9},{11,1... | collective-permute-start | bytes 73736 | tf_op jit(solution)/shard_map/ppermute | solution.py:10
  261.9 55.8 %collective-permute-start.29 = (f32[24,256]{1,0:T(8,128)}, f32[24,256]{1,0:T(8,128)S(1)}, u32[]{:S(2)}, u32[]{:S(2)}) collective-permute-start(f32[24,256]{1,0:T(8,128)} %get-tuple-element.27), channel_id=1, source_target_pairs={{65,0},{66,1},{67,2},{68,3},{69,4},{70,5},{71,6},{72,7},{73,8},{74... | collective-permute-start | bytes 73736 | tf_op jit(solution)/shard_map/ppermute | solution.py:10
  263.8 29.5 %collective-permute-start.26 = (f32[24,256]{1,0:T(8,128)}, f32[24,256]{1,0:T(8,128)S(1)}, u32[]{:S(2)}, u32[]{:S(2)}) collective-permute-start(f32[24,256]{1,0:T(8,128)} %get-tuple-element.30), channel_id=1, source_target_pairs={{73,0},{74,1},{75,2},{76,3},{77,4},{78,5},{79,6},{80,7},{81,8},{82... | collective-permute-start | bytes 73736 | tf_op jit(solution)/shard_map/ppermute | solution.py:10
  280.1 21.8 %copy-start.11 = (f32[24,256]{1,0:T(8,128)S(1)}, f32[24,256]{1,0:T(8,128)}, u32[]{:S(2)}) copy-start(f32[24,256]{1,0:T(8,128)} %get-tuple-element.28) | copy-start | bytes 73732
  280.1 58.4 %copy-start.10 = (f32[24,256]{1,0:T(8,128)S(1)}, f32[24,256]{1,0:T(8,128)}, u32[]{:S(2)}) copy-start(f32[24,256]{1,0:T(8,128)} %get-tuple-element.23) | copy-start | bytes 73732
  280.1 66.9 %copy-start.9 = (f32[24,256]{1,0:T(8,128)S(1)}, f32[24,256]{1,0:T(8,128)}, u32[]{:S(2)}) copy-start(f32[24,256]{1,0:T(8,128)} %get-tuple-element.22) | copy-start | bytes 73732
  280.1 75.9 %copy-start.8 = (f32[24,256]{1,0:T(8,128)S(1)}, f32[24,256]{1,0:T(8,128)}, u32[]{:S(2)}) copy-start(f32[24,256]{1,0:T(8,128)} %get-tuple-element.21) | copy-start | bytes 73732
  280.1 85.2 %copy-start.7 = (f32[24,256]{1,0:T(8,128)S(1)}, f32[24,256]{1,0:T(8,128)}, u32[]{:S(2)}) copy-start(f32[24,256]{1,0:T(8,128)} %get-tuple-element.20) | copy-start | bytes 73732
  280.2 90.9 %copy-start.6 = (f32[24,256]{1,0:T(8,128)S(1)}, f32[24,256]{1,0:T(8,128)}, u32[]{:S(2)}) copy-start(f32[24,256]{1,0:T(8,128)} %get-tuple-element.19) | copy-start | bytes 73732
  280.2 103.8 %copy-start.5 = (f32[24,256]{1,0:T(8,128)S(1)}, f32[24,256]{1,0:T(8,128)}, u32[]{:S(2)}) copy-start(f32[24,256]{1,0:T(8,128)} %get-tuple-element.18) | copy-start | bytes 73732
  280.2 113.4 %copy-start.4 = (f32[24,256]{1,0:T(8,128)S(1)}, f32[24,256]{1,0:T(8,128)}, u32[]{:S(2)}) copy-start(f32[24,256]{1,0:T(8,128)} %get-tuple-element.17) | copy-start | bytes 73732
  280.2 125.1 %copy-start.3 = (f32[24,256]{1,0:T(8,128)S(1)}, f32[24,256]{1,0:T(8,128)}, u32[]{:S(2)}) copy-start(f32[24,256]{1,0:T(8,128)} %get-tuple-element.16) | copy-start | bytes 73732
  280.2 136.8 %copy-start.2 = (f32[24,256]{1,0:T(8,128)S(1)}, f32[24,256]{1,0:T(8,128)}, u32[]{:S(2)}) copy-start(f32[24,256]{1,0:T(8,128)} %get-tuple-element.15) | copy-start | bytes 73732
  280.2 145.9 %copy-start.1 = (f32[24,256]{1,0:T(8,128)S(1)}, f32[24,256]{1,0:T(8,128)}, u32[]{:S(2)}) copy-start(f32[24,256]{1,0:T(8,128)} %get-tuple-element.14) | copy-start | bytes 73732
  293.3 8.6 %collective-permute-start.27 = (f32[24,256]{1,0:T(8,128)S(1)}, f32[24,256]{1,0:T(8,128)S(1)}, u32[]{:S(2)}, u32[]{:S(2)}) collective-permute-start(f32[24,256]{1,0:T(8,128)S(1)} %copy-done.12), channel_id=1, source_target_pairs={{9,0},{10,1},{11,2},{12,3},{13,4},{14,5},{15,6},{16,7},{17,8},{18,... | collective-permute-start | bytes 73736 | tf_op jit(solution)/shard_map/ppermute | solution.py:10
  301.9 12.1 %collective-permute-start.28 = (f32[24,256]{1,0:T(8,128)S(1)}, f32[24,256]{1,0:T(8,128)S(1)}, u32[]{:S(2)}, u32[]{:S(2)}) collective-permute-start(f32[24,256]{1,0:T(8,128)S(1)} %copy-done.11), channel_id=1, source_target_pairs={{0,55},{1,56},{2,57},{3,58},{4,59},{5,60},{6,61},{7,62},{8,63},{9,... | collective-permute-start | bytes 73736 | tf_op jit(solution)/shard_map/ppermute | solution.py:10
  314.0 176.3 %collective-permute-start.51 = (f32[24,256]{1,0:T(8,128)S(1)}, f32[24,256]{1,0:T(8,128)S(1)}, u32[]{:S(2)}, u32[]{:S(2)}) collective-permute-start(f32[24,256]{1,0:T(8,128)S(1)} %get-tuple-element.5), channel_id=1, source_target_pairs={{0,73},{1,74},{2,75},{3,76},{4,77},{5,78},{6,79},{7,80},{8,81},{9,... | collective-permute-start | bytes 73736 | tf_op jit(solution)/shard_map/ppermute | solution.py:10
  317.7 172.6 %collective-permute-start.50 = (f32[24,256]{1,0:T(8,128)S(1)}, f32[24,256]{1,0:T(8,128)S(1)}, u32[]{:S(2)}, u32[]{:S(2)}) collective-permute-start(f32[24,256]{1,0:T(8,128)S(1)} %get-tuple-element.6), channel_id=1, source_target_pairs={{0,9},{1,10},{2,11},{3,12},{4,13},{5,14},{6,15},{7,16},{8,17},{9,1... | collective-permute-start | bytes 73736 | tf_op jit(solution)/shard_map/ppermute | solution.py:10
  322.0 168.3 %collective-permute-start.49 = (f32[24,256]{1,0:T(8,128)S(1)}, f32[24,256]{1,0:T(8,128)S(1)}, u32[]{:S(2)}, u32[]{:S(2)}) collective-permute-start(f32[24,256]{1,0:T(8,128)S(1)} %get-tuple-element.7), channel_id=1, source_target_pairs={{55,0},{56,1},{57,2},{58,3},{59,4},{60,5},{61,6},{62,7},{63,8},{64... | collective-permute-start | bytes 73736 | tf_op jit(solution)/shard_map/ppermute | solution.py:10
  336.6 153.7 %collective-permute-start.48 = (f32[24,256]{1,0:T(8,128)S(1)}, f32[24,256]{1,0:T(8,128)S(1)}, u32[]{:S(2)}, u32[]{:S(2)}) collective-permute-start(f32[24,256]{1,0:T(8,128)S(1)} %get-tuple-element.8), channel_id=1, source_target_pairs={{0,65},{1,66},{2,67},{3,68},{4,69},{5,70},{6,71},{7,72},{8,73},{9,... | collective-permute-start | bytes 73736 | tf_op jit(solution)/shard_map/ppermute | solution.py:10
  338.6 8.5 %collective-permute-start.33 = (f32[24,256]{1,0:T(8,128)S(1)}, f32[24,256]{1,0:T(8,128)S(1)}, u32[]{:S(2)}, u32[]{:S(2)}) collective-permute-start(f32[24,256]{1,0:T(8,128)S(1)} %copy-done.10), channel_id=1, source_target_pairs={{0,7},{1,8},{2,9},{3,10},{4,11},{5,12},{6,13},{7,14},{8,15},{9,16}... | collective-permute-start | bytes 73736 | tf_op jit(solution)/shard_map/ppermute | solution.py:10
  347.0 9.0 %collective-permute-start.34 = (f32[24,256]{1,0:T(8,128)S(1)}, f32[24,256]{1,0:T(8,128)S(1)}, u32[]{:S(2)}, u32[]{:S(2)}) collective-permute-start(f32[24,256]{1,0:T(8,128)S(1)} %copy-done.9), channel_id=1, source_target_pairs={{0,71},{1,72},{2,73},{3,74},{4,75},{5,76},{6,77},{7,78},{8,79},{9,... | collective-permute-start | bytes 73736 | tf_op jit(solution)/shard_map/ppermute | solution.py:10
  356.1 9.2 %collective-permute-start.35 = (f32[24,256]{1,0:T(8,128)S(1)}, f32[24,256]{1,0:T(8,128)S(1)}, u32[]{:S(2)}, u32[]{:S(2)}) collective-permute-start(f32[24,256]{1,0:T(8,128)S(1)} %copy-done.8), channel_id=1, source_target_pairs={{72,0},{73,1},{74,2},{75,3},{76,4},{77,5},{78,6},{79,7},{80,8},{81... | collective-permute-start | bytes 73736 | tf_op jit(solution)/shard_map/ppermute | solution.py:10
  365.3 5.7 %collective-permute-start.36 = (f32[24,256]{1,0:T(8,128)S(1)}, f32[24,256]{1,0:T(8,128)S(1)}, u32[]{:S(2)}, u32[]{:S(2)}) collective-permute-start(f32[24,256]{1,0:T(8,128)S(1)} %copy-done.7), channel_id=1, source_target_pairs={{8,0},{9,1},{10,2},{11,3},{12,4},{13,5},{14,6},{15,7},{16,8},{17,9... | collective-permute-start | bytes 73736 | tf_op jit(solution)/shard_map/ppermute | solution.py:10
  371.0 12.9 %collective-permute-start.37 = (f32[24,256]{1,0:T(8,128)S(1)}, f32[24,256]{1,0:T(8,128)S(1)}, u32[]{:S(2)}, u32[]{:S(2)}) collective-permute-start(f32[24,256]{1,0:T(8,128)S(1)} %copy-done.6), channel_id=1, source_target_pairs={{0,56},{1,57},{2,58},{3,59},{4,60},{5,61},{6,62},{7,63},{8,64},{9,... | collective-permute-start | bytes 73736 | tf_op jit(solution)/shard_map/ppermute | solution.py:10
  384.0 9.6 %collective-permute-start.38 = (f32[24,256]{1,0:T(8,128)S(1)}, f32[24,256]{1,0:T(8,128)S(1)}, u32[]{:S(2)}, u32[]{:S(2)}) collective-permute-start(f32[24,256]{1,0:T(8,128)S(1)} %copy-done.5), channel_id=1, source_target_pairs={{64,0},{65,1},{66,2},{67,3},{68,4},{69,5},{70,6},{71,7},{72,8},{73... | collective-permute-start | bytes 73736 | tf_op jit(solution)/shard_map/ppermute | solution.py:10
  393.6 11.7 %collective-permute-start.39 = (f32[24,256]{1,0:T(8,128)S(1)}, f32[24,256]{1,0:T(8,128)S(1)}, u32[]{:S(2)}, u32[]{:S(2)}) collective-permute-start(f32[24,256]{1,0:T(8,128)S(1)} %copy-done.4), channel_id=1, source_target_pairs={{0,64},{1,65},{2,66},{3,67},{4,68},{5,69},{6,70},{7,71},{8,72},{9,... | collective-permute-start | bytes 73736 | tf_op jit(solution)/shard_map/ppermute | solution.py:10
  405.3 11.7 %collective-permute-start.40 = (f32[24,256]{1,0:T(8,128)S(1)}, f32[24,256]{1,0:T(8,128)S(1)}, u32[]{:S(2)}, u32[]{:S(2)}) collective-permute-start(f32[24,256]{1,0:T(8,128)S(1)} %copy-done.3), channel_id=1, source_target_pairs={{56,0},{57,1},{58,2},{59,3},{60,4},{61,5},{62,6},{63,7},{64,8},{65... | collective-permute-start | bytes 73736 | tf_op jit(solution)/shard_map/ppermute | solution.py:10
  417.0 9.0 %collective-permute-start.41 = (f32[24,256]{1,0:T(8,128)S(1)}, f32[24,256]{1,0:T(8,128)S(1)}, u32[]{:S(2)}, u32[]{:S(2)}) collective-permute-start(f32[24,256]{1,0:T(8,128)S(1)} %copy-done.2), channel_id=1, source_target_pairs={{0,8},{1,9},{2,10},{3,11},{4,12},{5,13},{6,14},{7,15},{8,16},{9,17... | collective-permute-start | bytes 73736 | tf_op jit(solution)/shard_map/ppermute | solution.py:10
  426.1 9.6 %collective-permute-start.42 = (f32[24,256]{1,0:T(8,128)S(1)}, f32[24,256]{1,0:T(8,128)S(1)}, u32[]{:S(2)}, u32[]{:S(2)}) collective-permute-start(f32[24,256]{1,0:T(8,128)S(1)} %copy-done.1), channel_id=1, source_target_pairs={{0,72},{1,73},{2,74},{3,75},{4,76},{5,77},{6,78},{7,79},{8,80},{9,... | collective-permute-start | bytes 73736 | tf_op jit(solution)/shard_map/ppermute | solution.py:10
  435.7 11.2 %collective-permute-start.43 = (f32[24,256]{1,0:T(8,128)S(1)}, f32[24,256]{1,0:T(8,128)S(1)}, u32[]{:S(2)}, u32[]{:S(2)}) collective-permute-start(f32[24,256]{1,0:T(8,128)S(1)} %get-tuple-element.13), channel_id=1, source_target_pairs={{71,0},{72,1},{73,2},{74,3},{75,4},{76,5},{77,6},{78,7},{79,8},{80... | collective-permute-start | bytes 73736 | tf_op jit(solution)/shard_map/ppermute | solution.py:10
  446.8 6.3 %collective-permute-start.44 = (f32[24,256]{1,0:T(8,128)S(1)}, f32[24,256]{1,0:T(8,128)S(1)}, u32[]{:S(2)}, u32[]{:S(2)}) collective-permute-start(f32[24,256]{1,0:T(8,128)S(1)} %get-tuple-element.12), channel_id=1, source_target_pairs={{7,0},{8,1},{9,2},{10,3},{11,4},{12,5},{13,6},{14,7},{15,8},{16,9}... | collective-permute-start | bytes 73736 | tf_op jit(solution)/shard_map/ppermute | solution.py:10
  453.2 13.3 %collective-permute-start.45 = (f32[24,256]{1,0:T(8,128)S(1)}, f32[24,256]{1,0:T(8,128)S(1)}, u32[]{:S(2)}, u32[]{:S(2)}) collective-permute-start(f32[24,256]{1,0:T(8,128)S(1)} %get-tuple-element.11), channel_id=1, source_target_pairs={{0,57},{1,58},{2,59},{3,60},{4,61},{5,62},{6,63},{7,64},{8,65},{9,... | collective-permute-start | bytes 73736 | tf_op jit(solution)/shard_map/ppermute | solution.py:10
  466.5 13.3 %collective-permute-start.46 = (f32[24,256]{1,0:T(8,128)S(1)}, f32[24,256]{1,0:T(8,128)S(1)}, u32[]{:S(2)}, u32[]{:S(2)}) collective-permute-start(f32[24,256]{1,0:T(8,128)S(1)} %get-tuple-element.10), channel_id=1, source_target_pairs={{63,0},{64,1},{65,2},{66,3},{67,4},{68,5},{69,6},{70,7},{71,8},{72... | collective-permute-start | bytes 73736 | tf_op jit(solution)/shard_map/ppermute | solution.py:10
  479.7 10.6 %collective-permute-start.47 = (f32[24,256]{1,0:T(8,128)S(1)}, f32[24,256]{1,0:T(8,128)S(1)}, u32[]{:S(2)}, u32[]{:S(2)}) collective-permute-start(f32[24,256]{1,0:T(8,128)S(1)} %get-tuple-element.9), channel_id=1, source_target_pairs={{0,1},{1,2},{2,3},{3,4},{4,5},{5,6},{6,7},{7,8},{8,9},{9,10},{10,1... | collective-permute-start | bytes 73736 | tf_op jit(solution)/shard_map/ppermute | solution.py:10
  (3 other events, 39.2 us)
where the time goes:
time: 499 us; the launch traced here: 497 us
  starting transfers between devices  225 us (45%)
  waiting for transfers between devices  207 us (41%)
  other arithmetic  43.8 us (9%)
  local copies, waits for them, and re-layouts  9.11 us (2%)
  matrix products  9.1 us (2%)
    ppermute x52, starting transfers between devices, passed_along(): return lax.ppermute(block, axis, route)  225 us
    ppermute x52, waiting for transfers between devices, passed_along(): return lax.ppermute(block, axis, route)  207 us
    scatter-add x1, other arithmetic, local(): mirror_sum = jax.ops.segment_sum(mirror_rows, source_ids, source_rows)  13.1 us
    scatter-add x1, other arithmetic, local(): local_sum = jax.ops.segment_sum(forward_rows, target_ids, box_count)  13.1 us
  transfers between devices with their start and end apart: 52, of which 34 were waited for; matrix products, arithmetic and copies ran while one was open for 10% of the time, Pallas kernels for 0%

commit v1 on v0

v1 whole, which is shorter than its diff:
```python
import functools

import jax
import jax.numpy as jnp
from jax import lax
from jax.experimental import pallas as pl
from jax.experimental.pallas import tpu as pltpu
from jax.sharding import PartitionSpec as P

MESH = pl.DeviceIdType.MESH
F32 = jnp.float32
BF16 = jnp.bfloat16
I32 = jnp.int32

BOXES = 64
POINTS = 256
PAIRS = 1024
LANES = 26
SLOTS = 24
OPS = 16
OWN = 13
ROWS = 80
WINDOW = 64


def code_of(lane):
    return lane if lane < OWN else lane + 1


def heading(code):
    return code // 9 - 1, code // 3 % 3 - 1, code % 3 - 1


def iota(shape, axis):
    return lax.broadcasted_iota(I32, shape, axis)


def one_hot(condition):
    return jnp.where(condition, 1.0, 0.0).astype(BF16)


def nt(a, b):
    return lax.dot_general(a, b, (((1,), (1,)), ((), ())), preferred_element_type=F32)


def mm(a, b):
    return jnp.dot(a, b, preferred_element_type=F32)


def pack_block(count, pairs_ref, send_ref, m_ref, block, meta):
    source = pairs_ref[0:1, :]
    target = pairs_ref[1:2, :]
    operator = pairs_ref[2:3, :]
    used = iota((1, PAIRS), 1) < count
    ghost = jnp.maximum(source - BOXES, 0)
    lane = jnp.right_shift(ghost * 2731, 16)
    slot = ghost - lane * SLOTS
    lane = jnp.where(used, jnp.where(source < BOXES, LANES, lane), 31)
    codes = iota((32, PAIRS), 0)
    start = jnp.sum(jnp.where(lane < codes, 1.0, 0.0), axis=1, keepdims=True)
    before = one_hot(iota((128, 128), 0) < iota((128, 128), 1))
    carry = start
    places = []
    for chunk in range(PAIRS // 128):
        hot = jnp.where(codes[:, :128] == lane[:, chunk * 128:(chunk + 1) * 128], 1.0, 0.0)
        rank = mm(hot.astype(BF16), before) + carry
        places.append(jnp.sum(hot * rank, axis=0, keepdims=True))
        carry = carry + jnp.sum(hot, axis=1, keepdims=True)
    place = jnp.concatenate(places, axis=1).astype(I32)
    fields = jnp.concatenate(
        [slot, target, operator, jnp.zeros((5, PAIRS), I32)], axis=0
    ).astype(F32).astype(BF16)
    for q in range(4):
        hot = one_hot(iota((256, PAIRS), 0) + 256 * q == place)
        ordered = nt(fields, hot)
        meta[4 * q:4 * q + 3, :] = ordered[0:3, :]
    sends = send_ref[...].astype(F32)
    for q in range(3):
        meta[4 * q + 3:4 * q + 4, :] = sends[:, 256 * q:256 * q + 256]
    diagonal = iota((32, 128), 0) == iota((32, 128), 1)
    starts = jnp.sum(jnp.where(diagonal, start, 0.0), axis=0, keepdims=True).astype(I32)
    high = jnp.right_shift(starts, 5)
    meta[15:16, 0:128] = high.astype(F32)
    meta[15:16, 128:256] = (starts - high * 32).astype(F32)
    block[0:BOXES, :] = m_ref[...]
    block[BOXES:ROWS, :] = meta[...].astype(BF16)


def exchange_kernel(nx, ny, nz, count_ref, pairs_ref, send_ref, m_ref, out_ref, meta, send_sem, recv_sem):
    g = lax.axis_index("gx")
    h = lax.axis_index("gy")
    by = lax.rem(g, ny)
    bz = lax.div(g, ny)
    steps = {
        "z": {1: bz < nz - 1, -1: bz > 0, 0: True},
        "y": {1: by < ny - 1, -1: by > 0, 0: True},
        "x": {1: h < nx - 1, -1: h > 0, 0: True},
    }
    partner = {
        "z": lambda s: (g + s * ny, h),
        "y": lambda s: (g + s, h),
        "x": lambda s: (g, h + s),
    }

    def on_grid(dx, dy, dz):
        cond = None
        for flag in (steps["x"][dx], steps["y"][dy], steps["z"][dz]):
            if flag is not True:
                cond = flag if cond is None else jnp.logical_and(cond, flag)
        return cond

    barrier = pltpu.get_barrier_semaphore()
    for axis in "zyx":
        for s in (1, -1):
            @pl.when(steps[axis][s])
            def _():
                pl.semaphore_signal(barrier, inc=1, device_id=partner[axis](s), device_id_type=MESH)

    pack_block(count_ref[0], pairs_ref, send_ref, m_ref, out_ref.at[OWN], meta)

    for code in range(27):
        if code != OWN:
            @pl.when(jnp.logical_not(on_grid(*heading(code))))
            def _():
                out_ref[code] = jnp.zeros((ROWS, POINTS), BF16)

    pl.semaphore_wait(
        barrier,
        sum(steps[axis][s].astype(I32) for axis in "zyx" for s in (1, -1)),
    )

    def as_code(dx, dy, dz):
        return (dx + 1) * 9 + (dy + 1) * 3 + dz + 1

    started = []

    def send(src, axis, s):
        dx, dy, dz = src
        dst = {"x": (-s, dy, dz), "y": (dx, -s, dz), "z": (dx, dy, -s)}[axis]
        need = {"x": (s, dy, dz), "y": (dx, s, dz), "z": (dx, dy, s)}[axis]
        cond = on_grid(*need)
        copy = pltpu.make_async_remote_copy(
            src_ref=out_ref.at[as_code(*src)],
            dst_ref=out_ref.at[as_code(*dst)],
            send_sem=send_sem.at[len(started)],
            recv_sem=recv_sem.at[as_code(*dst)],
            device_id=partner[axis](s),
            device_id_type=MESH,
        )
        started.append((copy, cond))
        pl.when(cond)(copy.start)

    def arrived(where):
        code = as_code(*where)
        slot = out_ref.at[code]
        copy = pltpu.make_async_remote_copy(
            src_ref=slot, dst_ref=slot, send_sem=send_sem.at[0], recv_sem=recv_sem.at[code],
            device_id=(g, h), device_id_type=MESH,
        )
        pl.when(on_grid(*where))(copy.wait_recv)

    home = (0, 0, 0)
    for axis in "zyx":
        for s in (1, -1):
            send(home, axis, s)
    for where in [(0, 1, 0), (0, -1, 0)]:
        arrived(where)
        for s in (1, -1):
            send(where, "x", s)
    for where in [(0, 0, 1), (0, 0, -1)]:
        arrived(where)
        for axis in "yx":
            for s in (1, -1):
                send(where, axis, s)
    for where in [(0, 1, 1), (0, -1, 1), (0, 1, -1), (0, -1, -1)]:
        arrived(where)
        for s in (1, -1):
            send(where, "x", s)
    for code in range(27):
        if heading(code)[0] != 0:
            arrived(heading(code))
    for copy, cond in started:
        pl.when(cond)(copy.wait_send)


def column(row):
    n = row.shape[1]
    parts = []
    for c in range(n // 128):
        piece = jnp.broadcast_to(row[:, c * 128:(c + 1) * 128], (8, 128))
        parts.append(jnp.transpose(piece)[:, 0:1])
    return jnp.concatenate(parts, axis=0)


def compute_kernel(count_ref, pairs_ref, blocks, ops_ref, out_ref, meta, starts_v, starts_s, events, ghost, rows_f, rows_m, keys_m, zm, copy_sem):
    for code in range(27):
        wide = blocks[code, BOXES:ROWS, :].astype(F32)
        for q in range(4):
            meta[code, q, 0:4, :] = wide[4 * q:4 * q + 4, :]
            meta[code, q, 4:8, :] = wide[4 * q:4 * q + 4, :]
        starts_v[code:code + 1, :] = (wide[15:16, 0:128] * 32.0 + wide[15:16, 128:256]).astype(I32)
    copy = pltpu.make_async_copy(starts_v, starts_s, copy_sem)
    copy.start()

    source = pairs_ref[0:1, :]
    target = pairs_ref[1:2, :]
    operator = pairs_ref[2:3, :]
    used = iota((1, PAIRS), 1) < count_ref[0]
    key_f = jnp.where(used, operator * BOXES + target, -1)
    keys_m[0:1, 0:PAIRS] = jnp.where(
        jnp.logical_and(used, source < BOXES), operator * BOXES + source, -1
    )
    boxes = []
    for q in range(3):
        flat = iota((1, 256), 1) + 256 * q
        row = jnp.full((1, 256), -1.0, F32)
        for lane in range(LANES):
            low = lane * SLOTS
            if low < 256 * (q + 1) and low + SLOTS > 256 * q:
                mine = jnp.logical_and(flat >= low, flat < low + SLOTS)
                row = jnp.where(mine, meta[code_of(lane), q, 3:4, :], row)
        boxes.append(row)
    box_column = column(jnp.concatenate(boxes, axis=1)).astype(I32)
    own_boxes = column(
        jnp.concatenate([meta[OWN, q, 3:4, :] for q in range(3)], axis=1)
    )
    copy.wait()

    across = iota((8, 128), 1)

    def window(code, begin, offset):
        begin = jnp.minimum(begin, PAIRS - 1)
        chunk = lax.div(begin, 128)
        after = jnp.minimum(chunk + 1, 7)

        def piece(c):
            return meta[code, lax.div(c, 2), :, pl.ds(pl.multiple_of(lax.rem(c, 2) * 128, 128), 128)]

        shift = begin - chunk * 128
        turn = lax.rem(256 + offset - shift, 128)
        first = pltpu.roll(piece(chunk), turn, 1)
        second = pltpu.roll(piece(after), turn, 1)
        return jnp.where(across < 128 - shift + offset, first, second)

    def own_box(slots, lane_boxes):
        hot = iota((SLOTS, 128), 0) == slots.astype(I32)
        return jnp.sum(jnp.where(hot, lane_boxes, 0.0), axis=0, keepdims=True)

    def lane_span(code, back):
        begin = starts_s[code, back]
        return begin, starts_s[code, back + 1] - begin

    for pair in range(LANES // 2):
        halves = []
        for half in range(2):
            lane = 2 * pair + half
            code, back = code_of(lane), LANES - 1 - lane
            begin, count = lane_span(code, back)
            part = window(code, begin, 64 * half)
            box = own_box(part[0:1, :], own_boxes[back * SLOTS:(back + 1) * SLOTS, :])
            key = (part[2:3, :] * BOXES + box).astype(I32)
            key = jnp.where(across[0:1, :] - 64 * half < count, key, -1)
            halves.append((part, key))
        low = across < 64
        events[:, pair * 128:(pair + 1) * 128] = jnp.where(low, halves[0][0], halves[1][0])
        keys_m[0:1, PAIRS + pair * 128:PAIRS + (pair + 1) * 128] = jnp.where(
            low[0:1, :], halves[0][1], halves[1][1]
        )

    ghost[0:BOXES, :] = blocks[OWN, 0:BOXES, :]
    ghost[BOXES + LANES * SLOTS:, :] = jnp.zeros((768 - BOXES - LANES * SLOTS, POINTS), BF16)
    for group in range(7):
        lanes = list(range(4 * group, min(4 * group + 4, LANES)))
        width = 64 * len(lanes)
        base = group * 256
        table = jnp.concatenate([blocks[code_of(lane), 0:BOXES, :] for lane in lanes], axis=0)
        targets = column(events[1:2, base:base + width]).astype(I32)
        which = jnp.right_shift(iota((width, 1), 0), 6)
        hot = one_hot(iota((width, width), 1) == targets + 64 * which)
        rows_m[PAIRS + base:PAIRS + base + width, :] = mm(hot, table).astype(BF16)
        picks = []
        for i, lane in enumerate(lanes):
            picked = box_column[lane * SLOTS:(lane + 1) * SLOTS, :] + 64 * i
            picks.append(jnp.where(iota((SLOTS, width), 1) == picked, 1.0, 0.0))
        hot = jnp.concatenate(picks, axis=0).astype(BF16)
        first = BOXES + SLOTS * lanes[0]
        ghost[first:first + SLOTS * len(lanes), :] = mm(hot, table).astype(BF16)

    source_column = column(source.astype(F32)).astype(I32)
    target_column = column(target.astype(F32)).astype(I32)
    for q in range(4):
        span = slice(q * 256, (q + 1) * 256)
        hot = one_hot(iota((256, 768), 1) == source_column[span, :])
        rows_f[span, :] = mm(hot, ghost[...]).astype(BF16)
        hot = one_hot(iota((256, BOXES), 1) == target_column[span, :])
        rows_m[span, :] = mm(hot, blocks[OWN, 0:BOXES, :]).astype(BF16)

    width_m = PAIRS + LANES * 64

    zm[...] = jnp.zeros_like(zm)

    @pl.loop(0, LANES)
    def _(lane):
        code = jnp.where(lane < OWN, lane, lane + 1)
        back = LANES - 1 - lane
        begin, count = lane_span(code, back)

        @pl.loop(1, lax.div(count + WINDOW - 1, WINDOW))
        def _(turn):
            part = window(code, begin + turn * WINDOW, 0)
            flat = iota((1, 128), 1)
            boxes_row = jnp.zeros((1, 128), F32)
            slots = part[0:1, :].astype(I32) + back * SLOTS
            for q in range(6):
                spread = own_boxes[q * 128:(q + 1) * 128, :]
                hot = iota((128, 128), 0) + 128 * q == slots
                boxes_row += jnp.sum(jnp.where(hot, spread, 0.0), axis=0, keepdims=True)
            key = (part[2:3, :] * BOXES + boxes_row).astype(I32)
            left = jnp.minimum(count - turn * WINDOW, WINDOW)
            key = jnp.where(flat < left, key, -1)
            hot = one_hot(iota((128, BOXES), 1) == column(part[1:2, :]).astype(I32))
            rows = mm(hot, blocks[code, 0:BOXES, :]).astype(BF16)
            for q in range(4):
                hot = one_hot(iota((256, 128), 0) + 256 * q == key)
                zm[256 * q:256 * (q + 1), :] += mm(hot, rows)

    total = jnp.zeros((128, POINTS), F32)
    for q in range(4):
        hot = one_hot(iota((256, PAIRS), 0) + 256 * q == key_f)
        forward = mm(hot, rows_f[...])
        hot = one_hot(iota((256, width_m), 0) + 256 * q == keys_m[...])
        mirror = mm(hot, rows_m[...]) + zm[256 * q:256 * (q + 1), :]
        f_high = forward.astype(BF16)
        f_low = (forward - f_high.astype(F32)).astype(BF16)
        m_high = mirror.astype(BF16)
        m_low = (mirror - m_high.astype(F32)).astype(BF16)
        for i in range(4):
            part = slice(64 * i, 64 * i + 64)
            matrix = ops_ref[4 * q + i]
            total += mm(jnp.concatenate([f_high[part], f_low[part]], axis=0), matrix)
            total += nt(jnp.concatenate([m_high[part], m_low[part]], axis=0), matrix)
    out_ref[...] = total[0:BOXES, :] + total[BOXES:, :]


def local(sizes, multipoles, operators, pairs, pair_count, send_list):
    nx, ny, nz = sizes
    vmem = pl.BlockSpec(memory_space=pltpu.VMEM)
    smem = pl.BlockSpec(memory_space=pltpu.SMEM)
    sends = jnp.pad(send_list, (0, 768 - LANES * SLOTS)).reshape(1, 768)
    blocks = pl.pallas_call(
        functools.partial(exchange_kernel, nx, ny, nz),
        out_shape=jax.ShapeDtypeStruct((27, ROWS, POINTS), BF16),
        in_specs=[smem, vmem, vmem, vmem],
        out_specs=vmem,
        scratch_shapes=[
            pltpu.VMEM((16, 256), F32),
            pltpu.SemaphoreType.DMA((26,)),
            pltpu.SemaphoreType.DMA((27,)),
        ],
        compiler_params=pltpu.CompilerParams(
            collective_id=0, has_side_effects=True, vmem_limit_bytes=32 * 1024 * 1024
        ),
        name="exchange",
    )(pair_count, pairs, sends, multipoles)
    width_m = PAIRS + LANES * 64
    return pl.pallas_call(
        compute_kernel,
        out_shape=jax.ShapeDtypeStruct((BOXES, POINTS), F32),
        in_specs=[smem, vmem, vmem, vmem],
        out_specs=vmem,
        scratch_shapes=[
            pltpu.VMEM((27, 4, 8, 256), F32),
            pltpu.VMEM((27, 128), I32),
            pltpu.SMEM((27, 128), I32),
            pltpu.VMEM((8, LANES * 64), F32),
            pltpu.VMEM((768, POINTS), BF16),
            pltpu.VMEM((PAIRS, POINTS), BF16),
            pltpu.VMEM((width_m, POINTS), BF16),
            pltpu.VMEM((1, width_m), I32),
            pltpu.VMEM((1024, POINTS), F32),
            pltpu.SemaphoreType.DMA,
        ],
        compiler_params=pltpu.CompilerParams(vmem_limit_bytes=48 * 1024 * 1024),
        name="compute",
    )(pair_count, pairs, blocks, operators)


def solution(mesh):
    shape = dict(mesh.shape)
    ny = min(8, shape["gx"] // 2)
    sizes = (shape["gy"], ny, shape["gx"] // ny)
    return jax.shard_map(
        functools.partial(local, sizes),
        mesh=mesh,
        in_specs=(
            P(("gx", "gy"), None),
            P(),
            P(None, ("gx", "gy")),
            P(("gx", "gy")),
            P(("gx", "gy")),
        ),
        out_specs=P(("gx", "gy"), None),
        check_vma=False,
    )
```

time: 499 us -> 45.5 us (0.09)
  the two profiles are of different devices: /device:TPU:32 before, /device:TPU:43 now
where the time goes in v1:
time: 45.5 us; the launch traced here: 45.2 us
  Pallas kernels  40 us (88%)
  local copies, waits for them, and re-layouts  4.48 us (10%)
  between operations  0.67 us (1%)
    pallas_call x1, Pallas kernels, local(): pl.pallas_call(functools.partial(exchange_kernel, nx, ny, nz), out_shape=...  31.9 us
    pallas_call x1, Pallas kernels, local(): pl.pallas_call(compute_kernel, out_shape=jax.ShapeDtypeStruct((BOXES, POI...  8.08 us
    unnamed x8, local copies, waits for them, and re-layouts  3.78 us

profile of v1, /device:TPU:43, one launch (start us, length us, event | category | flops | bytes accessed | tf_op | source)
XLA Modules:
  0.0 45.2 jit_solution(2550410108708334272)
XLA Ops:
  0.7 0.7 %pad.4 = s32[768]{0:T(1024)S(1)} pad(s32[624]{0:T(1024)} %param.9, s32[]{:T(128)} %constant.0.clone.1), padding=0_144 | pad | bytes 5572 | tf_op jit(solution)/shard_map/jit(_pad)/pad | solution.py:349
  1.4 0.0 copy-start.1
  1.4 0.7 %copy-done.1 = s32[3,1024]{1,0:T(4,128)S(1)} copy-done((s32[3,1024]{1,0:T(4,128)S(1)}, s32[3,1024]{1,0:T(4,128)}, u32[]{:S(2)}) %copy-start.1) | copy-done | bytes 12312
  2.1 0.0 copy-start.3
  2.1 0.8 %copy-done.3 = bf16[64,256]{1,0:T(8,128)(2,1)S(1)} copy-done((bf16[64,256]{1,0:T(8,128)(2,1)S(1)}, bf16[64,256]{1,0:T(8,128)(2,1)}, u32[]{:S(2)}) %copy-start.3) | copy-done | bytes 32792
  2.8 31.9 %exchange.1.blocks = bf16[27,80,256]{2,1,0:T(8,128)(2,1)S(1)} custom-call(s32[1]{0:T(128)S(6)} %copy.6.count_ref, s32[3,1024]{1,0:T(4,128)S(1)} %copy-done.1, s32[1,768]{1,0:T(1,128)S(1)} %reshape.3.send_ref, bf16[64,256]{1,0:T(8,128)(2,1)S(1)} %copy-done.3), custom_call_target="tpu_custom_call" | custom-call | tf_op jit(solution)/shard_map/exchange/pallas_call | solution.py:350
  34.8 0.0 copy-start
  34.8 1.6 %copy-done = bf16[16,256,256]{2,1,0:T(8,128)(2,1)S(1)} copy-done((bf16[16,256,256]{2,1,0:T(8,128)(2,1)S(1)}, bf16[16,256,256]{2,1,0:T(8,128)(2,1)}, u32[]{:S(2)}) %copy-start) | copy-done | bytes 2097176
  36.4 0.0 copy-start.2
  36.4 0.7 %copy-done.2 = s32[3,1024]{1,0:T(4,128)S(1)} copy-done((s32[3,1024]{1,0:T(4,128)S(1)}, s32[3,1024]{1,0:T(4,128)}, u32[]{:S(2)}) %copy-start.2) | copy-done | bytes 12312
  37.1 8.1 %compute.1 = f32[64,256]{1,0:T(8,128)} custom-call(s32[1]{0:T(128)S(6)} %copy.6.count_ref, s32[3,1024]{1,0:T(4,128)S(1)} %copy-done.2, bf16[27,80,256]{2,1,0:T(8,128)(2,1)S(1)} %exchange.1.blocks, bf16[16,256,256]{2,1,0:T(8,128)(2,1)S(1)} %copy-done), custom_call_target="tpu_custom_call" | custom-call | tf_op jit(solution)/shard_map/compute/pallas_call | solution.py:366
  (1 shorter events, 0.0 us)
Async XLA Ops:
  1.4 0.7 %copy-start.1 = (s32[3,1024]{1,0:T(4,128)S(1)}, s32[3,1024]{1,0:T(4,128)}, u32[]{:S(2)}) copy-start(s32[3,1024]{1,0:T(4,128)} %pairs_ref.3) | copy-start | bytes 36868
  2.1 0.8 %copy-start.3 = (bf16[64,256]{1,0:T(8,128)(2,1)S(1)}, bf16[64,256]{1,0:T(8,128)(2,1)}, u32[]{:S(2)}) copy-start(bf16[64,256]{1,0:T(8,128)(2,1)} %m_ref.1) | copy-start | bytes 98308
  34.8 1.6 %copy-start = (bf16[16,256,256]{2,1,0:T(8,128)(2,1)S(1)}, bf16[16,256,256]{2,1,0:T(8,128)(2,1)}, u32[]{:S(2)}) copy-start(bf16[16,256,256]{2,1,0:T(8,128)(2,1)} %ops_ref.1) | copy-start | bytes 6291460
  36.4 0.7 %copy-start.2 = (s32[3,1024]{1,0:T(4,128)S(1)}, s32[3,1024]{1,0:T(4,128)}, u32[]{:S(2)}) copy-start(s32[3,1024]{1,0:T(4,128)} %pairs_ref.3) | copy-start | bytes 36868

commit v2 on v0

v2 whole, which is shorter than its diff:
```python
import functools

import jax
import jax.numpy as jnp
from jax import lax
from jax.experimental import pallas as pl
from jax.experimental.pallas import tpu as pltpu
from jax.sharding import PartitionSpec as P

MESH = pl.DeviceIdType.MESH
F32 = jnp.float32
BF16 = jnp.bfloat16
I32 = jnp.int32

BOXES = 64
POINTS = 256
PAIRS = 1024
LANES = 26
SLOTS = 24
OPS = 16
OWN = 13
ROWS = 80
WINDOW = 64


ORDER = list(range(9, 17)) + list(range(0, 9)) + list(range(17, 26))
GROUPS = [ORDER[0:4], ORDER[4:8], ORDER[8:12], ORDER[12:16], ORDER[16:20], ORDER[20:24], ORDER[24:26]]
EARLY = 2


def code_of(lane):
    return lane if lane < OWN else lane + 1


def heading(code):
    return code // 9 - 1, code // 3 % 3 - 1, code % 3 - 1


def iota(shape, axis):
    return lax.broadcasted_iota(I32, shape, axis)


def one_hot(condition):
    return jnp.where(condition, 1.0, 0.0).astype(BF16)


def nt(a, b):
    return lax.dot_general(a, b, (((1,), (1,)), ((), ())), preferred_element_type=F32)


def mm(a, b):
    return jnp.dot(a, b, preferred_element_type=F32)


def pack_pairs(count, pairs_ref, send_ref, tail, meta):
    source = pairs_ref[0:1, :]
    target = pairs_ref[1:2, :]
    operator = pairs_ref[2:3, :]
    used = iota((1, PAIRS), 1) < count
    ghost = jnp.maximum(source - BOXES, 0)
    lane = jnp.right_shift(ghost * 2731, 16)
    slot = ghost - lane * SLOTS
    lane = jnp.where(used, jnp.where(source < BOXES, LANES, lane), 31)
    codes = iota((32, PAIRS), 0)
    start = jnp.sum(jnp.where(lane < codes, 1.0, 0.0), axis=1, keepdims=True)
    before = one_hot(iota((128, 128), 0) < iota((128, 128), 1))
    carry = start
    places = []
    for chunk in range(PAIRS // 128):
        hot = jnp.where(codes[:, :128] == lane[:, chunk * 128:(chunk + 1) * 128], 1.0, 0.0)
        rank = mm(hot.astype(BF16), before) + carry
        places.append(jnp.sum(hot * rank, axis=0, keepdims=True))
        carry = carry + jnp.sum(hot, axis=1, keepdims=True)
    place = jnp.concatenate(places, axis=1).astype(I32)
    fields = jnp.concatenate(
        [slot, target, operator, jnp.zeros((5, PAIRS), I32)], axis=0
    ).astype(F32).astype(BF16)
    for q in range(4):
        hot = one_hot(iota((256, PAIRS), 0) + 256 * q == place)
        ordered = nt(fields, hot)
        meta[4 * q:4 * q + 3, :] = ordered[0:3, :]
    sends = send_ref[...].astype(F32)
    meta[3:4, :] = sends[:, 0:256]
    meta[7:8, :] = sends[:, 256:512]
    meta[11:12, 0:112] = sends[:, 512:624]
    meta[11:12, 112:256] = jnp.zeros((1, 144), F32)
    diagonal = iota((32, 128), 0) == iota((32, 128), 1)
    starts = jnp.sum(jnp.where(diagonal, start, 0.0), axis=0, keepdims=True).astype(I32)
    high = jnp.right_shift(starts, 5)
    meta[15:16, 0:128] = high.astype(F32)
    meta[15:16, 128:256] = (starts - high * 32).astype(F32)
    tail[...] = meta[...].astype(BF16)


def split(value):
    high = value.astype(BF16)
    return high, (value - high.astype(F32)).astype(BF16)


def count_own(count, pairs_ref, own_counts, hot_t):
    source = pairs_ref[0:1, :]
    target = pairs_ref[1:2, :]
    operator = pairs_ref[2:3, :]
    used = jnp.logical_and(iota((1, PAIRS), 1) < count, source < BOXES)
    key = jnp.where(used, operator * BOXES + source, -1)
    hot_t[...] = one_hot(iota((BOXES, PAIRS), 0) == target)
    for q in range(4):
        hot = one_hot(iota((256, PAIRS), 0) + 256 * q == key)
        high, low = split(nt(hot, hot_t[...]))
        own_counts[256 * q:256 * (q + 1), :] = jnp.concatenate([high, low], axis=1)


def count_forward(count, pairs_ref, counts, hot_u):
    source = pairs_ref[0:1, :]
    target = pairs_ref[1:2, :]
    operator = pairs_ref[2:3, :]
    used = iota((1, PAIRS), 1) < count
    key = jnp.where(used, operator * BOXES + target, -1)
    low, high = BOXES + 9 * SLOTS, BOXES + 17 * SLOTS
    moved = jnp.where(source < low, source + 8 * SLOTS, jnp.where(source < high, source - 9 * SLOTS, source))
    hot_u[...] = one_hot(iota((768, PAIRS), 0) == jnp.where(source < BOXES, source, moved))
    for q in range(4):
        hot = one_hot(iota((256, PAIRS), 0) + 256 * q == key)
        for c in range(3):
            high, low = split(nt(hot, hot_u[256 * c:256 * (c + 1), :]))
            counts[256 * q:256 * (q + 1), 256 * c:256 * (c + 1)] = high
            counts[256 * q:256 * (q + 1), 768 + 256 * c:768 + 256 * (c + 1)] = low


def column(row):
    n = row.shape[1]
    parts = []
    for c in range(n // 128):
        piece = jnp.broadcast_to(row[:, c * 128:(c + 1) * 128], (8, 128))
        parts.append(jnp.transpose(piece)[:, 0:1])
    return jnp.concatenate(parts, axis=0)


def unpack(blocks, code, meta, starts_v):
    wide = blocks[code, BOXES:ROWS, :].astype(F32)
    for q in range(4):
        meta[code, q, 0:4, :] = wide[4 * q:4 * q + 4, :]
        meta[code, q, 4:8, :] = wide[4 * q:4 * q + 4, :]
    starts_v[code:code + 1, :] = (wide[15:16, 0:128] * 32.0 + wide[15:16, 128:256]).astype(I32)


def longest_lane(starts):
    lengths = pltpu.roll(starts, 127, 1) - starts
    code = iota((32, 128), 0)
    back = LANES - 1 - jnp.where(code < OWN, code, code - 1)
    theirs = jnp.logical_and(iota((32, 128), 1) == back, jnp.logical_and(code != OWN, code < 27))
    lengths = jnp.where(theirs, lengths, 0).astype(F32)
    return jnp.max(jnp.max(lengths, axis=0, keepdims=True), axis=1, keepdims=True)


def window(meta, code, begin, offset):
    begin = jnp.minimum(begin, PAIRS - 1)
    chunk = lax.div(begin, 128)
    after = jnp.minimum(chunk + 1, 7)

    def piece(c):
        return meta[code, lax.div(c, 2), :, pl.ds(pl.multiple_of(lax.rem(c, 2) * 128, 128), 128)]

    shift = begin - chunk * 128
    turn = lax.rem(256 + offset - shift, 128)
    first = pltpu.roll(piece(chunk), turn, 1)
    second = pltpu.roll(piece(after), turn, 1)
    return jnp.where(iota((8, 128), 1) < 128 - shift + offset, first, second)


def gather_ghosts(blocks, group, meta, ghost):
    width = 64 * len(group)
    table = jnp.concatenate([blocks[code_of(lane), 0:BOXES, :] for lane in group], axis=0)
    picks = []
    for i, lane in enumerate(group):
        low = lane * SLOTS
        q, at = low // 128, low % 128
        cells = [meta[code_of(lane), p // 2, 3:4, p % 2 * 128:p % 2 * 128 + 128] for p in (q, min(q + 1, 5))]
        both = column(jnp.concatenate(cells, axis=1))
        picked = both[at:at + SLOTS, :].astype(I32) + 64 * i
        picks.append(jnp.where(iota((SLOTS, width), 1) == picked, 1.0, 0.0))
    hot = jnp.concatenate(picks, axis=0).astype(BF16)
    first = BOXES + SLOTS * ORDER.index(group[0])
    ghost[first:first + SLOTS * len(group), :] = mm(hot, table).astype(BF16)


def gather_events(blocks, group, meta, starts_v, own_boxes, events, keys_m, rows_m):
    base = 64 * ORDER.index(group[0])
    across = iota((8, 128), 1)
    upper = iota((8, 128), 0) < 4
    left = across < 64

    def pick(first, second):
        return jnp.where(upper, first, second)

    for pair in range(len(group) // 2):
        codes = [code_of(lane) for lane in group[2 * pair:2 * pair + 2]]
        backs = [LANES - 1 - lane for lane in group[2 * pair:2 * pair + 2]]
        start = [starts_v[c:c + 1, b:b + 1] for c, b in zip(codes, backs)]
        after = [starts_v[c:c + 1, b + 1:b + 2] for c, b in zip(codes, backs)]
        begin = jnp.minimum(pick(*start), PAIRS - 1)
        offset = pick(jnp.int32(0), jnp.int32(64))
        chunk = jnp.right_shift(begin, 7)
        shift = begin - chunk * 128
        chunks = [
            pick(*[meta[c, p // 2, :, p % 2 * 128:p % 2 * 128 + 128] for c in codes]) for p in range(8)
        ]
        now, later = chunks[0], chunks[1]
        for p in range(1, 8):
            here = chunk == p
            now = jnp.where(here, chunks[p], now)
            later = jnp.where(here, chunks[min(p + 1, 7)], later)
        amount = jnp.bitwise_and(shift - offset + 128, 127)
        for bit in range(7):
            turned = jnp.bitwise_and(amount, 1 << bit) != 0
            now = jnp.where(turned, pltpu.roll(now, 128 - (1 << bit), 1), now)
            later = jnp.where(turned, pltpu.roll(later, 128 - (1 << bit), 1), later)
        part = jnp.where(across < 128 - shift + offset, now, later)
        part = jnp.where(left, part, pltpu.roll(part, 4, 0))
        hot = iota((SLOTS, 128), 0) == part[0:1, :].astype(I32)
        theirs = [own_boxes[b * SLOTS:(b + 1) * SLOTS, :] for b in backs]
        theirs = jnp.where(iota((SLOTS, 128), 1) < 64, *theirs)
        box = jnp.sum(jnp.where(hot, theirs, 0.0), axis=0, keepdims=True)
        key = (part[2:3, :] * BOXES + box).astype(I32)
        flat = iota((1, 128), 1)
        length = jnp.where(flat < 64, after[0] - start[0], after[1] - start[1])
        span = slice(base + pair * 128, base + (pair + 1) * 128)
        events[:, span] = part
        keys_m[0:1, span] = jnp.where(jnp.where(flat < 64, flat, flat - 64) < length, key, -1)
    width = 64 * len(group)
    table = jnp.concatenate([blocks[code_of(lane), 0:BOXES, :] for lane in group], axis=0)
    targets = column(events[1:2, base:base + width]).astype(I32)
    which = jnp.right_shift(iota((width, 1), 0), 6)
    hot = one_hot(iota((width, width), 1) == targets + 64 * which)
    rows_m[base:base + width, :] = mm(hot, table).astype(BF16)


def apply_operators(total, forward, mirror, ops_ref, q):
    if forward is not None:
        f_high, f_low = split(forward)
    m_high, m_low = split(mirror)
    for i in range(4):
        part = slice(64 * i, 64 * i + 64)
        matrix = ops_ref[4 * q + i]
        if forward is not None:
            total += mm(jnp.concatenate([f_high[part], f_low[part]], axis=0), matrix)
        total += nt(jnp.concatenate([m_high[part], m_low[part]], axis=0), matrix)
    return total


def remainder_kernel(field_hbm, blocks_hbm, ops_hbm, out_hbm, field, blocks, ops_ref, meta, starts_v, starts_s, zm, sem):
    fetch = pltpu.make_async_copy(field_hbm.at[pl.ds(BOXES, 8)], field.at[pl.ds(BOXES, 8)], sem.at[0])
    through = pltpu.make_async_copy(field_hbm.at[pl.ds(0, BOXES)], out_hbm, sem.at[1])
    fetch.start()
    through.start()
    fetch.wait()
    through.wait()

    @pl.when(jnp.max(field[BOXES:, :]) > WINDOW)
    def _():
        loads = [
            pltpu.make_async_copy(field_hbm, field, sem.at[0]),
            pltpu.make_async_copy(blocks_hbm, blocks, sem.at[1]),
            pltpu.make_async_copy(ops_hbm, ops_ref, sem.at[2]),
        ]
        for load in loads:
            load.start()
        for load in loads:
            load.wait()
        for code in range(27):
            unpack(blocks, code, meta, starts_v)
        copy = pltpu.make_async_copy(starts_v, starts_s, sem.at[3])
        copy.start()
        copy.wait()
        own_boxes = column(jnp.concatenate([meta[OWN, q, 3:4, :] for q in range(3)], axis=1))
        zm[...] = jnp.zeros_like(zm)

        @pl.loop(0, LANES)
        def _(lane):
            code = jnp.where(lane < OWN, lane, lane + 1)
            back = LANES - 1 - lane
            begin = starts_s[code, back]
            length = starts_s[code, back + 1] - begin

            @pl.loop(1, lax.div(length + WINDOW - 1, WINDOW))
            def _(turn):
                part = window(meta, code, begin + turn * WINDOW, 0)
                boxes_row = jnp.zeros((1, 128), F32)
                slots = part[0:1, :].astype(I32) + back * SLOTS
                for q in range(6):
                    hot = iota((128, 128), 0) + 128 * q == slots
                    spread = own_boxes[q * 128:(q + 1) * 128, :]
                    boxes_row += jnp.sum(jnp.where(hot, spread, 0.0), axis=0, keepdims=True)
                key = (part[2:3, :] * BOXES + boxes_row).astype(I32)
                key = jnp.where(iota((1, 128), 1) < jnp.minimum(length - turn * WINDOW, WINDOW), key, -1)
                hot = one_hot(iota((128, BOXES), 1) == column(part[1:2, :]).astype(I32))
                rows = mm(hot, blocks[code, 0:BOXES, :]).astype(BF16)
                for q in range(4):
                    hot = one_hot(iota((256, 128), 0) + 256 * q == key)
                    zm[256 * q:256 * (q + 1), :] += mm(hot, rows)

        total = jnp.zeros((128, POINTS), F32)
        for q in range(4):
            total = apply_operators(total, None, zm[256 * q:256 * (q + 1), :], ops_ref, q)
        field[0:BOXES, :] += total[0:BOXES, :] + total[BOXES:, :]
        store = pltpu.make_async_copy(field.at[pl.ds(0, BOXES)], out_hbm, sem.at[1])
        store.start()
        store.wait()


def main_kernel(
    nx, ny, nz, count_ref, pairs_hbm, send_hbm, m_hbm, ops_hbm,
    field_ref, blocks_hbm,
    blocks, ops_ref, counts, own_counts, pairs_ref, send_ref, tail, hot_t, hot_u,
    meta, starts_v, events, keys_m, ghost, rows_m, zf, zm,
    in_sem, send_sem, recv_sem,
):
    g = lax.axis_index("gx")
    h = lax.axis_index("gy")
    by = lax.rem(g, ny)
    bz = lax.div(g, ny)
    steps = {
        "z": {1: bz < nz - 1, -1: bz > 0, 0: True},
        "y": {1: by < ny - 1, -1: by > 0, 0: True},
        "x": {1: h < nx - 1, -1: h > 0, 0: True},
    }
    partner = {
        "z": lambda s: (g + s * ny, h),
        "y": lambda s: (g + s, h),
        "x": lambda s: (g, h + s),
    }

    def on_grid(dx, dy, dz):
        cond = None
        for flag in (steps["x"][dx], steps["y"][dy], steps["z"][dz]):
            if flag is not True:
                cond = flag if cond is None else jnp.logical_and(cond, flag)
        return cond

    barrier = pltpu.get_barrier_semaphore()
    for axis in "zyx":
        for s in (1, -1):
            @pl.when(steps[axis][s])
            def _():
                pl.semaphore_signal(barrier, inc=1, device_id=partner[axis](s), device_id_type=MESH)

    loads = [
        pltpu.make_async_copy(src, dst, in_sem.at[i])
        for i, (src, dst) in enumerate([
            (pairs_hbm, pairs_ref),
            (send_hbm, send_ref),
            (m_hbm, blocks.at[OWN, pl.ds(0, BOXES)]),
            (ops_hbm, ops_ref),
        ])
    ]
    for load in loads:
        load.start()

    pl.semaphore_wait(
        barrier,
        sum(steps[axis][s].astype(I32) for axis in "zyx" for s in (1, -1)),
    )

    def as_code(dx, dy, dz):
        return (dx + 1) * 9 + (dy + 1) * 3 + dz + 1

    spans = [pl.ds(0, BOXES), pl.ds(BOXES, ROWS - BOXES)]
    started = []

    def send(src, axis, s, part):
        dx, dy, dz = src
        dst = {"x": (-s, dy, dz), "y": (dx, -s, dz), "z": (dx, dy, -s)}[axis]
        need = {"x": (s, dy, dz), "y": (dx, s, dz), "z": (dx, dy, s)}[axis]
        cond = on_grid(*need)
        own = src == (0, 0, 0) and part == 0
        copy = pltpu.make_async_remote_copy(
            src_ref=m_hbm if own else blocks.at[as_code(*src), spans[part]],
            dst_ref=blocks.at[as_code(*dst), spans[part]],
            send_sem=send_sem.at[len(started)],
            recv_sem=recv_sem.at[part, as_code(*dst)],
            device_id=partner[axis](s),
            device_id_type=MESH,
        )
        started.append((copy, cond))
        pl.when(cond)(copy.start)

    def arrived(where, part):
        code = as_code(*where)
        slot = blocks.at[code, spans[part]]
        copy = pltpu.make_async_remote_copy(
            src_ref=slot, dst_ref=slot, send_sem=send_sem.at[0], recv_sem=recv_sem.at[part, code],
            device_id=(g, h), device_id_type=MESH,
        )
        pl.when(on_grid(*where))(copy.wait_recv)

    def send_home(part):
        for axis in "zyx":
            for s in (1, -1):
                send((0, 0, 0), axis, s, part)

    def relay(places, axes, part):
        for where in places:
            arrived(where, part)
            for axis in axes:
                for s in (1, -1):
                    send(where, axis, s, part)

    along_y = [(0, 1, 0), (0, -1, 0)]
    along_z = [(0, 0, 1), (0, 0, -1)]
    along_yz = [(0, 1, 1), (0, -1, 1), (0, 1, -1), (0, -1, -1)]
    count = count_ref[0]
    send_home(0)
    loads[0].wait()
    loads[1].wait()
    pack_pairs(count, pairs_ref, send_ref, blocks.at[OWN, spans[1]], tail)
    send_home(1)
    for code in range(27):
        if code != OWN:
            @pl.when(jnp.logical_not(on_grid(*heading(code))))
            def _():
                blocks[code] = jnp.zeros((ROWS, POINTS), BF16)
    starts_v[27:32, :] = jnp.zeros((5, 128), I32)
    ghost[BOXES + LANES * SLOTS:, :] = jnp.zeros((768 - BOXES - LANES * SLOTS, POINTS), BF16)
    own_boxes = column(
        jnp.concatenate([tail[4 * q + 3:4 * q + 4, :] for q in range(3)], axis=1)
    )
    count_own(count, pairs_ref, own_counts, hot_t)
    count_forward(count, pairs_ref, counts, hot_u)
    relay(along_y, "x", 0)
    relay(along_z, "yx", 0)
    relay(along_y, "x", 1)
    relay(along_z, "yx", 1)
    relay(along_yz, "x", 0)
    relay(along_yz, "x", 1)
    loads[2].wait()
    loads[3].wait()

    def take(groups):
        for lane in sum(groups, []):
            unpack(blocks, code_of(lane), meta, starts_v)
        for group in groups:
            gather_ghosts(blocks, group, meta, ghost)
        for group in groups:
            gather_events(blocks, group, meta, starts_v, own_boxes, events, keys_m, rows_m)

    ghost[0:BOXES, :] = blocks[OWN, 0:BOXES, :]
    starts_v[0:27, :] = jnp.zeros((27, 128), I32)
    take(GROUPS[:EARLY])
    own = blocks[OWN, 0:BOXES, :]
    own_twice = jnp.concatenate([own, own], axis=0)
    cut = EARLY * 256
    quarters = [slice(256 * q, 256 * (q + 1)) for q in range(4)]
    for q, span in enumerate(quarters):
        zf[span, :] = mm(counts[span, 0:256], ghost[0:256, :]) + mm(counts[span, 768:1024], ghost[0:256, :])
        hot = one_hot(iota((256, cut), 0) + 256 * q == keys_m[:, 0:cut])
        zm[span, :] = mm(hot, rows_m[0:cut, :]) + mm(own_counts[span, :], own_twice)

    for part in range(2):
        for code in range(27):
            if heading(code)[0] != 0:
                arrived(heading(code), part)
    save = pltpu.make_async_copy(blocks, blocks_hbm, in_sem.at[4])
    save.start()
    take(GROUPS[EARLY:])
    total = jnp.zeros((128, POINTS), F32)
    for q, span in enumerate(quarters):
        forward = zf[span, :] + mm(counts[span, 256:768], ghost[256:768, :])
        forward += mm(counts[span, 1024:1536], ghost[256:768, :])
        hot = one_hot(iota((256, LANES * 64 - cut), 0) + 256 * q == keys_m[:, cut:])
        mirror = zm[span, :] + mm(hot, rows_m[cut:, :])
        total = apply_operators(total, forward, mirror, ops_ref, q)
    field_ref[0:BOXES, :] = total[0:BOXES, :] + total[BOXES:, :]
    field_ref[BOXES:, :] = jnp.full((8, POINTS), 0.0, F32) + longest_lane(starts_v[...])
    save.wait()
    for copy, cond in started:
        pl.when(cond)(copy.wait_send)


def local(sizes, multipoles, operators, pairs, pair_count, send_list):
    nx, ny, nz = sizes
    smem = pl.BlockSpec(memory_space=pltpu.SMEM)
    vmem = pl.BlockSpec(memory_space=pltpu.VMEM)
    anywhere = pl.BlockSpec(memory_space=pl.ANY)
    blocks_shape = (27, ROWS, POINTS)
    field, blocks = pl.pallas_call(
        functools.partial(main_kernel, nx, ny, nz),
        out_shape=[
            jax.ShapeDtypeStruct((BOXES + 8, POINTS), F32),
            jax.ShapeDtypeStruct(blocks_shape, BF16),
        ],
        in_specs=[smem, anywhere, anywhere, anywhere, anywhere],
        out_specs=[vmem, anywhere],
        scratch_shapes=[
            pltpu.VMEM(blocks_shape, BF16),
            pltpu.VMEM((OPS, POINTS, POINTS), BF16),
            pltpu.VMEM((1024, 1536), BF16),
            pltpu.VMEM((1024, 128), BF16),
            pltpu.VMEM((3, PAIRS), I32),
            pltpu.VMEM((1, LANES * SLOTS), I32),
            pltpu.VMEM((16, 256), F32),
            pltpu.VMEM((BOXES, PAIRS), BF16),
            pltpu.VMEM((768, PAIRS), BF16),
            pltpu.VMEM((27, 4, 8, 256), F32),
            pltpu.VMEM((32, 128), I32),
            pltpu.VMEM((8, LANES * 64), F32),
            pltpu.VMEM((1, LANES * 64), I32),
            pltpu.VMEM((768, POINTS), BF16),
            pltpu.VMEM((LANES * 64, POINTS), BF16),
            pltpu.VMEM((1024, POINTS), F32),
            pltpu.VMEM((1024, POINTS), F32),
            pltpu.SemaphoreType.DMA((5,)),
            pltpu.SemaphoreType.DMA((52,)),
            pltpu.SemaphoreType.DMA((2, 27)),
        ],
        compiler_params=pltpu.CompilerParams(
            collective_id=0, has_side_effects=True, vmem_limit_bytes=58 * 1024 * 1024
        ),
        name="exchange",
    )(pair_count, pairs, send_list.reshape(1, LANES * SLOTS), multipoles, operators)
    return pl.pallas_call(
        remainder_kernel,
        out_shape=jax.ShapeDtypeStruct((BOXES, POINTS), F32),
        in_specs=[anywhere] * 3,
        out_specs=anywhere,
        scratch_shapes=[
            pltpu.VMEM((BOXES + 8, POINTS), F32),
            pltpu.VMEM(blocks_shape, BF16),
            pltpu.VMEM((OPS, POINTS, POINTS), BF16),
            pltpu.VMEM((27, 4, 8, 256), F32),
            pltpu.VMEM((32, 128), I32),
            pltpu.SMEM((32, 128), I32),
            pltpu.VMEM((1024, POINTS), F32),
            pltpu.SemaphoreType.DMA((4,)),
        ],
        compiler_params=pltpu.CompilerParams(vmem_limit_bytes=58 * 1024 * 1024),
        name="remainder",
    )(field, blocks, operators)


def solution(mesh):
    shape = dict(mesh.shape)
    ny = min(8, shape["gx"] // 2)
    sizes = (shape["gy"], ny, shape["gx"] // ny)
    return jax.shard_map(
        functools.partial(local, sizes),
        mesh=mesh,
        in_specs=(
            P(("gx", "gy"), None),
            P(),
            P(None, ("gx", "gy")),
            P(("gx", "gy")),
            P(("gx", "gy")),
        ),
        out_specs=P(("gx", "gy"), None),
        check_vma=False,
    )
```

time: 499 us -> 43.6 us (0.09)
  the two profiles are of different devices: /device:TPU:32 before, /device:TPU:41 now
where the time goes in v2:
time: 43.6 us; the launch traced here: 43.3 us
  Pallas kernels  41.4 us (95%)
  local copies, waits for them, and re-layouts  1.27 us (3%)
  between operations  0.66 us (2%)
    pallas_call x1, Pallas kernels, local(): pl.pallas_call(functools.partial(main_kernel, nx, ny, nz), out_shape=[jax...  38.1 us
    pallas_call x1, Pallas kernels, local(): pl.pallas_call(remainder_kernel, out_shape=jax.ShapeDtypeStruct((BOXES, P...  3.24 us
    reshape x1, local copies, waits for them, and re-layouts, local(): send_list.reshape(1, LANES * SLOTS)  1.27 us

profile of v2, /device:TPU:41, one launch (start us, length us, event | category | flops | bytes accessed | tf_op | source)
XLA Modules:
  0.0 43.3 jit_solution(8120966167648492967)
XLA Ops:
  0.7 1.3 %reshape.3.send_hbm = s32[1,624]{1,0:T(1,128)} reshape(s32[624]{0:T(1024)} %param.9) | data formatting | bytes 4992 | tf_op jit(solution)/shard_map/reshape | solution.py:519
  1.9 38.1 %exchange.1 = (f32[72,256]{1,0:T(8,128)}, bf16[27,80,256]{2,1,0:T(8,128)(2,1)}) custom-call(s32[1]{0:T(128)S(6)} %copy.6.count_ref, s32[3,1024]{1,0:T(4,128)} %pairs_hbm.1, s32[1,624]{1,0:T(1,128)} %reshape.3.send_hbm, bf16[64,256]{1,0:T(8,128)(2,1)} %m_hbm.1, bf16[16,256,256]{2,1,0:T(8,128)(2,1)} %ops_hbm.3), custom_call_target="tpu_custom_call" | custom-call | tf_op jit(solution)/shard_map/exchange/pallas_call | solution.py:485
  40.1 3.2 %remainder.1 = f32[64,256]{1,0:T(8,128)} custom-call(f32[72,256]{1,0:T(8,128)} %get-tuple-element.7.field_hbm, bf16[27,80,256]{2,1,0:T(8,128)(2,1)} %get-tuple-element.8.blocks_hbm, bf16[16,256,256]{2,1,0:T(8,128)(2,1)} %ops_hbm.3), custom_call_target="tpu_custom_call" | custom-call | tf_op jit(solution)/shard_map/remainder/pallas_call | solution.py:520

commit v3 on v2

--- a/solution.py
+++ b/solution.py
@@ -23,9 +23,19 @@
 WINDOW = 64
 
 
-ORDER = list(range(9, 17)) + list(range(0, 9)) + list(range(17, 26))
-GROUPS = [ORDER[0:4], ORDER[4:8], ORDER[8:12], ORDER[12:16], ORDER[16:20], ORDER[20:24], ORDER[24:26]]
-EARLY = 2
+EARLY = [9, 10, 11, 12, 13, 14, 15, 16]
+MIDDLE = [4, 21, 1, 3, 5, 7, 18, 20, 22, 24]
+CORNERS = [0, 2, 6, 8, 17, 19, 23, 25]
+ORDER = EARLY + MIDDLE + CORNERS
+MID, LATE = 64 * len(EARLY), 64 * len(EARLY + MIDDLE)
+
+
+def quads(lanes):
+    return [lanes[i:i + 4] for i in range(0, len(lanes), 4)]
+
+
+def ghost_row(lane):
+    return BOXES + SLOTS * ORDER.index(lane) + (16 if lane in CORNERS else 0)
 
 
 def code_of(lane):
@@ -79,7 +89,7 @@
         hot = one_hot(iota((256, PAIRS), 0) + 256 * q == place)
         ordered = nt(fields, hot)
         meta[4 * q:4 * q + 3, :] = ordered[0:3, :]
-    sends = send_ref[...].astype(F32)
+    sends = send_ref[...].reshape(1, LANES * SLOTS).astype(F32)
     meta[3:4, :] = sends[:, 0:256]
     meta[7:8, :] = sends[:, 256:512]
     meta[11:12, 0:112] = sends[:, 512:624]
@@ -116,9 +126,11 @@
     operator = pairs_ref[2:3, :]
     used = iota((1, PAIRS), 1) < count
     key = jnp.where(used, operator * BOXES + target, -1)
-    low, high = BOXES + 9 * SLOTS, BOXES + 17 * SLOTS
-    moved = jnp.where(source < low, source + 8 * SLOTS, jnp.where(source < high, source - 9 * SLOTS, source))
-    hot_u[...] = one_hot(iota((768, PAIRS), 0) == jnp.where(source < BOXES, source, moved))
+    move = jnp.zeros((1, PAIRS), I32)
+    for lane in range(LANES):
+        first = BOXES + SLOTS * lane
+        move = jnp.where(source >= first, ghost_row(lane) - first, move)
+    hot_u[...] = one_hot(iota((768, PAIRS), 0) == source + move)
     for q in range(4):
         hot = one_hot(iota((256, PAIRS), 0) + 256 * q == key)
         for c in range(3):
@@ -180,7 +192,7 @@
         picked = both[at:at + SLOTS, :].astype(I32) + 64 * i
         picks.append(jnp.where(iota((SLOTS, width), 1) == picked, 1.0, 0.0))
     hot = jnp.concatenate(picks, axis=0).astype(BF16)
-    first = BOXES + SLOTS * ORDER.index(group[0])
+    first = ghost_row(group[0])
     ghost[first:first + SLOTS * len(group), :] = mm(hot, table).astype(BF16)
 
 
@@ -249,17 +261,13 @@
 
 
 def remainder_kernel(field_hbm, blocks_hbm, ops_hbm, out_hbm, field, blocks, ops_ref, meta, starts_v, starts_s, zm, sem):
-    fetch = pltpu.make_async_copy(field_hbm.at[pl.ds(BOXES, 8)], field.at[pl.ds(BOXES, 8)], sem.at[0])
-    through = pltpu.make_async_copy(field_hbm.at[pl.ds(0, BOXES)], out_hbm, sem.at[1])
+    fetch = pltpu.make_async_copy(field_hbm, field, sem.at[0])
     fetch.start()
-    through.start()
     fetch.wait()
-    through.wait()
 
     @pl.when(jnp.max(field[BOXES:, :]) > WINDOW)
     def _():
         loads = [
-            pltpu.make_async_copy(field_hbm, field, sem.at[0]),
             pltpu.make_async_copy(blocks_hbm, blocks, sem.at[1]),
             pltpu.make_async_copy(ops_hbm, ops_ref, sem.at[2]),
         ]
@@ -303,9 +311,10 @@
         for q in range(4):
             total = apply_operators(total, None, zm[256 * q:256 * (q + 1), :], ops_ref, q)
         field[0:BOXES, :] += total[0:BOXES, :] + total[BOXES:, :]
-        store = pltpu.make_async_copy(field.at[pl.ds(0, BOXES)], out_hbm, sem.at[1])
-        store.start()
-        store.wait()
+
+    store = pltpu.make_async_copy(field.at[pl.ds(0, BOXES)], out_hbm, sem.at[0])
+    store.start()
+    store.wait()
 
 
 def main_kernel(
@@ -420,7 +429,8 @@
             def _():
                 blocks[code] = jnp.zeros((ROWS, POINTS), BF16)
     starts_v[27:32, :] = jnp.zeros((5, 128), I32)
-    ghost[BOXES + LANES * SLOTS:, :] = jnp.zeros((768 - BOXES - LANES * SLOTS, POINTS), BF16)
+    ghost[496:512, :] = jnp.zeros((16, POINTS), BF16)
+    ghost[704:768, :] = jnp.zeros((64, POINTS), BF16)
     own_boxes = column(
         jnp.concatenate([tail[4 * q + 3:4 * q + 4, :] for q in range(3)], axis=1)
     )
@@ -435,40 +445,52 @@
     loads[2].wait()
     loads[3].wait()
 
-    def take(groups):
-        for lane in sum(groups, []):
+    def take(lanes):
+        for lane in lanes:
             unpack(blocks, code_of(lane), meta, starts_v)
-        for group in groups:
+        for group in quads(lanes):
             gather_ghosts(blocks, group, meta, ghost)
-        for group in groups:
+        for group in quads(lanes):
             gather_events(blocks, group, meta, starts_v, own_boxes, events, keys_m, rows_m)
+
+    def wait_for(lanes):
+        for part in range(2):
+            for lane in lanes:
+                arrived(heading(code_of(lane)), part)
+
+    def sums(q, low, high, first, last):
+        span = slice(256 * q, 256 * (q + 1))
+        forward = mm(counts[span, low:high], ghost[low:high, :])
+        forward += mm(counts[span, 768 + low:768 + high], ghost[low:high, :])
+        hot = one_hot(iota((256, last - first), 0) + 256 * q == keys_m[:, first:last])
+        return forward, mm(hot, rows_m[first:last, :])
 
     ghost[0:BOXES, :] = blocks[OWN, 0:BOXES, :]
     starts_v[0:27, :] = jnp.zeros((27, 128), I32)
-    take(GROUPS[:EARLY])
+    take(EARLY)
     own = blocks[OWN, 0:BOXES, :]
     own_twice = jnp.concatenate([own, own], axis=0)
-    cut = EARLY * 256
     quarters = [slice(256 * q, 256 * (q + 1)) for q in range(4)]
     for q, span in enumerate(quarters):
-        zf[span, :] = mm(counts[span, 0:256], ghost[0:256, :]) + mm(counts[span, 768:1024], ghost[0:256, :])
-        hot = one_hot(iota((256, cut), 0) + 256 * q == keys_m[:, 0:cut])
-        zm[span, :] = mm(hot, rows_m[0:cut, :]) + mm(own_counts[span, :], own_twice)
-
-    for part in range(2):
-        for code in range(27):
-            if heading(code)[0] != 0:
-                arrived(heading(code), part)
+        forward, mirror = sums(q, 0, 256, 0, MID)
+        zf[span, :] = forward
+        zm[span, :] = mirror + mm(own_counts[span, :], own_twice)
+
+    wait_for(MIDDLE)
+    take(MIDDLE)
+    for q, span in enumerate(quarters):
+        forward, mirror = sums(q, 256, 512, MID, LATE)
+        zf[span, :] += forward
+        zm[span, :] += mirror
+
+    wait_for(CORNERS)
     save = pltpu.make_async_copy(blocks, blocks_hbm, in_sem.at[4])
     save.start()
-    take(GROUPS[EARLY:])
+    take(CORNERS)
     total = jnp.zeros((128, POINTS), F32)
     for q, span in enumerate(quarters):
-        forward = zf[span, :] + mm(counts[span, 256:768], ghost[256:768, :])
-        forward += mm(counts[span, 1024:1536], ghost[256:768, :])
-        hot = one_hot(iota((256, LANES * 64 - cut), 0) + 256 * q == keys_m[:, cut:])
-        mirror = zm[span, :] + mm(hot, rows_m[cut:, :])
-        total = apply_operators(total, forward, mirror, ops_ref, q)
+        forward, mirror = sums(q, 512, 768, LATE, 64 * LANES)
+        total = apply_operators(total, zf[span, :] + forward, zm[span, :] + mirror, ops_ref, q)
     field_ref[0:BOXES, :] = total[0:BOXES, :] + total[BOXES:, :]
     field_ref[BOXES:, :] = jnp.full((8, POINTS), 0.0, F32) + longest_lane(starts_v[...])
     save.wait()
@@ -496,7 +518,7 @@
             pltpu.VMEM((1024, 1536), BF16),
             pltpu.VMEM((1024, 128), BF16),
             pltpu.VMEM((3, PAIRS), I32),
-            pltpu.VMEM((1, LANES * SLOTS), I32),
+            pltpu.VMEM((LANES * SLOTS,), I32),
             pltpu.VMEM((16, 256), F32),
             pltpu.VMEM((BOXES, PAIRS), BF16),
             pltpu.VMEM((768, PAIRS), BF16),
@@ -516,7 +538,7 @@
             collective_id=0, has_side_effects=True, vmem_limit_bytes=58 * 1024 * 1024
         ),
         name="exchange",
-    )(pair_count, pairs, send_list.reshape(1, LANES * SLOTS), multipoles, operators)
+    )(pair_count, pairs, send_list, multipoles, operators)
     return pl.pallas_call(
         remainder_kernel,
         out_shape=jax.ShapeDtypeStruct((BOXES, POINTS), F32),

time: 43.6 us -> 40.1 us (0.920)
  the two profiles are of different devices: /device:TPU:41 before, /device:TPU:46 now
where the time goes in v3:
time: 40.1 us; the launch traced here: 39.9 us
  Pallas kernels  39.2 us (98%)
  between operations  0.66 us (2%)
    pallas_call x1, Pallas kernels, local(): pl.pallas_call(functools.partial(main_kernel, nx, ny, nz), out_shape=[jax...  37.5 us
    pallas_call x1, Pallas kernels, local(): pl.pallas_call(remainder_kernel, out_shape=jax.ShapeDtypeStruct((BOXES, P...  1.67 us

profile of v3, /device:TPU:46, one launch (start us, length us, event | category | flops | bytes accessed | tf_op | source)
XLA Modules:
  0.0 39.9 jit_solution(17020795651624545988)
XLA Ops:
  0.7 37.5 %exchange.1 = (f32[72,256]{1,0:T(8,128)}, bf16[27,80,256]{2,1,0:T(8,128)(2,1)}) custom-call(s32[1]{0:T(128)S(6)} %copy.6.count_ref, s32[3,1024]{1,0:T(4,128)} %pairs_hbm.1, s32[624]{0:T(1024)} %send_hbm.1, bf16[64,256]{1,0:T(8,128)(2,1)} %m_hbm.1, bf16[16,256,256]{2,1,0:T(8,128)(2,1)} %ops_hbm.3), custom_call_target="tpu_custom_call" | custom-call | tf_op jit(solution)/shard_map/exchange/pallas_call | solution.py:507
  38.2 1.7 %remainder.1 = f32[64,256]{1,0:T(8,128)} custom-call(f32[72,256]{1,0:T(8,128)} %get-tuple-element.7.field_hbm, bf16[27,80,256]{2,1,0:T(8,128)(2,1)} %get-tuple-element.8.blocks_hbm, bf16[16,256,256]{2,1,0:T(8,128)(2,1)} %ops_hbm.3), custom_call_target="tpu_custom_call" | custom-call | tf_op jit(solution)/shard_map/remainder/pallas_call | solution.py:542

commit v4 on v3

--- a/solution.py
+++ b/solution.py
@@ -23,8 +23,8 @@
 WINDOW = 64
 
 
-EARLY = [9, 10, 11, 12, 13, 14, 15, 16]
-MIDDLE = [4, 21, 1, 3, 5, 7, 18, 20, 22, 24]
+EARLY = [1, 4, 7, 10, 15, 18, 21, 24]
+MIDDLE = [12, 13, 9, 11, 14, 16, 3, 5, 20, 22]
 CORNERS = [0, 2, 6, 8, 17, 19, 23, 25]
 ORDER = EARLY + MIDDLE + CORNERS
 MID, LATE = 64 * len(EARLY), 64 * len(EARLY + MIDDLE)
@@ -196,55 +196,61 @@
     ghost[first:first + SLOTS * len(group), :] = mm(hot, table).astype(BF16)
 
 
-def gather_events(blocks, group, meta, starts_v, own_boxes, events, keys_m, rows_m):
-    base = 64 * ORDER.index(group[0])
-    across = iota((8, 128), 1)
+def gather_events(blocks, lanes, meta, starts_v, own_boxes, events, keys_m, rows_m):
+    base = 64 * ORDER.index(lanes[0])
+    pairs = [lanes[i:i + 2] for i in range(0, len(lanes), 2)]
+    across = iota((8 * len(pairs), 128), 1)
     upper = iota((8, 128), 0) < 4
-    left = across < 64
-
-    def pick(first, second):
-        return jnp.where(upper, first, second)
-
-    for pair in range(len(group) // 2):
-        codes = [code_of(lane) for lane in group[2 * pair:2 * pair + 2]]
-        backs = [LANES - 1 - lane for lane in group[2 * pair:2 * pair + 2]]
-        start = [starts_v[c:c + 1, b:b + 1] for c, b in zip(codes, backs)]
-        after = [starts_v[c:c + 1, b + 1:b + 2] for c, b in zip(codes, backs)]
-        begin = jnp.minimum(pick(*start), PAIRS - 1)
-        offset = pick(jnp.int32(0), jnp.int32(64))
-        chunk = jnp.right_shift(begin, 7)
-        shift = begin - chunk * 128
-        chunks = [
-            pick(*[meta[c, p // 2, :, p % 2 * 128:p % 2 * 128 + 128] for c in codes]) for p in range(8)
-        ]
-        now, later = chunks[0], chunks[1]
-        for p in range(1, 8):
-            here = chunk == p
-            now = jnp.where(here, chunks[p], now)
-            later = jnp.where(here, chunks[min(p + 1, 7)], later)
-        amount = jnp.bitwise_and(shift - offset + 128, 127)
-        for bit in range(7):
-            turned = jnp.bitwise_and(amount, 1 << bit) != 0
-            now = jnp.where(turned, pltpu.roll(now, 128 - (1 << bit), 1), now)
-            later = jnp.where(turned, pltpu.roll(later, 128 - (1 << bit), 1), later)
-        part = jnp.where(across < 128 - shift + offset, now, later)
-        part = jnp.where(left, part, pltpu.roll(part, 4, 0))
-        hot = iota((SLOTS, 128), 0) == part[0:1, :].astype(I32)
-        theirs = [own_boxes[b * SLOTS:(b + 1) * SLOTS, :] for b in backs]
+
+    def stack(of_lane):
+        return jnp.concatenate(
+            [jnp.where(upper, of_lane(first), of_lane(second)) for first, second in pairs], axis=0
+        )
+
+    def start_of(lane, after):
+        code, back = code_of(lane), LANES - 1 - lane + after
+        return starts_v[code:code + 1, back:back + 1]
+
+    begin = jnp.minimum(stack(lambda lane: start_of(lane, 0)), PAIRS - 1)
+    offset = jnp.where(jnp.bitwise_and(iota(across.shape, 0), 4) == 0, 0, 64)
+    chunk = jnp.right_shift(begin, 7)
+    shift = begin - chunk * 128
+    chunks = [
+        stack(lambda lane: meta[code_of(lane), p // 2, :, p % 2 * 128:p % 2 * 128 + 128]) for p in range(8)
+    ]
+    now, later = chunks[0], chunks[1]
+    for p in range(1, 8):
+        here = chunk == p
+        now = jnp.where(here, chunks[p], now)
+        later = jnp.where(here, chunks[min(p + 1, 7)], later)
+    amount = jnp.bitwise_and(shift - offset + 128, 127)
+    for bit in range(7):
+        turned = jnp.bitwise_and(amount, 1 << bit) != 0
+        now = jnp.where(turned, pltpu.roll(now, 128 - (1 << bit), 1), now)
+        later = jnp.where(turned, pltpu.roll(later, 128 - (1 << bit), 1), later)
+    part = jnp.where(across < 128 - shift + offset, now, later)
+    flat = iota((1, 128), 1)
+    for i, (first, second) in enumerate(pairs):
+        fields = part[8 * i:8 * i + 8, :]
+        fields = jnp.where(flat < 64, fields, jnp.concatenate([fields[4:8, :], fields[0:4, :]], axis=0))
+        hot = iota((SLOTS, 128), 0) == fields[0:1, :].astype(I32)
+        theirs = [own_boxes[(LANES - 1 - lane) * SLOTS:(LANES - lane) * SLOTS, :] for lane in (first, second)]
         theirs = jnp.where(iota((SLOTS, 128), 1) < 64, *theirs)
         box = jnp.sum(jnp.where(hot, theirs, 0.0), axis=0, keepdims=True)
-        key = (part[2:3, :] * BOXES + box).astype(I32)
-        flat = iota((1, 128), 1)
-        length = jnp.where(flat < 64, after[0] - start[0], after[1] - start[1])
-        span = slice(base + pair * 128, base + (pair + 1) * 128)
-        events[:, span] = part
-        keys_m[0:1, span] = jnp.where(jnp.where(flat < 64, flat, flat - 64) < length, key, -1)
-    width = 64 * len(group)
-    table = jnp.concatenate([blocks[code_of(lane), 0:BOXES, :] for lane in group], axis=0)
-    targets = column(events[1:2, base:base + width]).astype(I32)
-    which = jnp.right_shift(iota((width, 1), 0), 6)
-    hot = one_hot(iota((width, width), 1) == targets + 64 * which)
-    rows_m[base:base + width, :] = mm(hot, table).astype(BF16)
+        key = (fields[2:3, :] * BOXES + box).astype(I32)
+        lengths = [start_of(lane, 1) - start_of(lane, 0) for lane in (first, second)]
+        key = jnp.where(jnp.where(flat < 64, flat, flat - 64) < jnp.where(flat < 64, *lengths), key, -1)
+        span = slice(base + i * 128, base + (i + 1) * 128)
+        events[:, span] = fields
+        keys_m[0:1, span] = key
+    for group in quads(lanes):
+        low = 64 * ORDER.index(group[0])
+        width = 64 * len(group)
+        table = jnp.concatenate([blocks[code_of(lane), 0:BOXES, :] for lane in group], axis=0)
+        targets = column(events[1:2, low:low + width]).astype(I32)
+        which = jnp.right_shift(iota((width, 1), 0), 6)
+        hot = one_hot(iota((width, width), 1) == targets + 64 * which)
+        rows_m[low:low + width, :] = mm(hot, table).astype(BF16)
 
 
 def apply_operators(total, forward, mirror, ops_ref, q):
@@ -365,15 +371,10 @@
     for load in loads:
         load.start()
 
-    pl.semaphore_wait(
-        barrier,
-        sum(steps[axis][s].astype(I32) for axis in "zyx" for s in (1, -1)),
-    )
-
     def as_code(dx, dy, dz):
         return (dx + 1) * 9 + (dy + 1) * 3 + dz + 1
 
-    spans = [pl.ds(0, BOXES), pl.ds(BOXES, ROWS - BOXES)]
+    spans = [pl.ds(0, ROWS)]
     started = []
 
     def send(src, axis, s, part):
@@ -381,7 +382,7 @@
         dst = {"x": (-s, dy, dz), "y": (dx, -s, dz), "z": (dx, dy, -s)}[axis]
         need = {"x": (s, dy, dz), "y": (dx, s, dz), "z": (dx, dy, s)}[axis]
         cond = on_grid(*need)
-        own = src == (0, 0, 0) and part == 0
+        own = False
         copy = pltpu.make_async_remote_copy(
             src_ref=m_hbm if own else blocks.at[as_code(*src), spans[part]],
             dst_ref=blocks.at[as_code(*dst), spans[part]],
@@ -418,11 +419,15 @@
     along_z = [(0, 0, 1), (0, 0, -1)]
     along_yz = [(0, 1, 1), (0, -1, 1), (0, 1, -1), (0, -1, -1)]
     count = count_ref[0]
-    send_home(0)
     loads[0].wait()
     loads[1].wait()
-    pack_pairs(count, pairs_ref, send_ref, blocks.at[OWN, spans[1]], tail)
-    send_home(1)
+    pack_pairs(count, pairs_ref, send_ref, blocks.at[OWN, pl.ds(BOXES, ROWS - BOXES)], tail)
+    loads[2].wait()
+    pl.semaphore_wait(
+        barrier,
+        sum(steps[axis][s].astype(I32) for axis in "zyx" for s in (1, -1)),
+    )
+    send_home(0)
     for code in range(27):
         if code != OWN:
             @pl.when(jnp.logical_not(on_grid(*heading(code))))
@@ -438,11 +443,6 @@
     count_forward(count, pairs_ref, counts, hot_u)
     relay(along_y, "x", 0)
     relay(along_z, "yx", 0)
-    relay(along_y, "x", 1)
-    relay(along_z, "yx", 1)
-    relay(along_yz, "x", 0)
-    relay(along_yz, "x", 1)
-    loads[2].wait()
     loads[3].wait()
 
     def take(lanes):
@@ -450,13 +450,12 @@
             unpack(blocks, code_of(lane), meta, starts_v)
         for group in quads(lanes):
             gather_ghosts(blocks, group, meta, ghost)
-        for group in quads(lanes):
-            gather_events(blocks, group, meta, starts_v, own_boxes, events, keys_m, rows_m)
+        gather_events(blocks, lanes, meta, starts_v, own_boxes, events, keys_m, rows_m)
 
     def wait_for(lanes):
-        for part in range(2):
-            for lane in lanes:
-                arrived(heading(code_of(lane)), part)
+        for lane in lanes:
+            if heading(code_of(lane))[0] != 0:
+                arrived(heading(code_of(lane)), 0)
 
     def sums(q, low, high, first, last):
         span = slice(256 * q, 256 * (q + 1))
@@ -467,6 +466,7 @@
 
     ghost[0:BOXES, :] = blocks[OWN, 0:BOXES, :]
     starts_v[0:27, :] = jnp.zeros((27, 128), I32)
+    wait_for(EARLY)
     take(EARLY)
     own = blocks[OWN, 0:BOXES, :]
     own_twice = jnp.concatenate([own, own], axis=0)
@@ -476,6 +476,7 @@
         zf[span, :] = forward
         zm[span, :] = mirror + mm(own_counts[span, :], own_twice)
 
+    relay(along_yz, "x", 0)
     wait_for(MIDDLE)
     take(MIDDLE)
     for q, span in enumerate(quarters):

time: 40.1 us -> 39.3 us (0.980)
  the two profiles are of different devices: /device:TPU:46 before, /device:TPU:43 now
where the time goes in v4:
time: 39.3 us; the launch traced here: 39.1 us
  Pallas kernels  38.4 us (98%)
  between operations  0.66 us (2%)
    pallas_call x1, Pallas kernels, local(): pl.pallas_call(functools.partial(main_kernel, nx, ny, nz), out_shape=[jax...  36.8 us
    pallas_call x1, Pallas kernels, local(): pl.pallas_call(remainder_kernel, out_shape=jax.ShapeDtypeStruct((BOXES, P...  1.67 us

profile of v4, /device:TPU:43, one launch (start us, length us, event | category | flops | bytes accessed | tf_op | source)
XLA Modules:
  0.0 39.1 jit_solution(5204873686413241777)
XLA Ops:
  0.7 36.8 %exchange.1 = (f32[72,256]{1,0:T(8,128)}, bf16[27,80,256]{2,1,0:T(8,128)(2,1)}) custom-call(s32[1]{0:T(128)S(6)} %copy.6.count_ref, s32[3,1024]{1,0:T(4,128)} %pairs_hbm.1, s32[624]{0:T(1024)} %send_hbm.1, bf16[64,256]{1,0:T(8,128)(2,1)} %m_hbm.1, bf16[16,256,256]{2,1,0:T(8,128)(2,1)} %ops_hbm.3), custom_call_target="tpu_custom_call" | custom-call | tf_op jit(solution)/shard_map/exchange/pallas_call | solution.py:508
  37.4 1.7 %remainder.1 = f32[64,256]{1,0:T(8,128)} custom-call(f32[72,256]{1,0:T(8,128)} %get-tuple-element.7.field_hbm, bf16[27,80,256]{2,1,0:T(8,128)(2,1)} %get-tuple-element.8.blocks_hbm, bf16[16,256,256]{2,1,0:T(8,128)(2,1)} %ops_hbm.3), custom_call_target="tpu_custom_call" | custom-call | tf_op jit(solution)/shard_map/remainder/pallas_call | solution.py:543

commit v5 on v4

--- a/solution.py
+++ b/solution.py
@@ -471,18 +471,13 @@
     own = blocks[OWN, 0:BOXES, :]
     own_twice = jnp.concatenate([own, own], axis=0)
     quarters = [slice(256 * q, 256 * (q + 1)) for q in range(4)]
-    for q, span in enumerate(quarters):
-        forward, mirror = sums(q, 0, 256, 0, MID)
-        zf[span, :] = forward
-        zm[span, :] = mirror + mm(own_counts[span, :], own_twice)
-
     relay(along_yz, "x", 0)
     wait_for(MIDDLE)
     take(MIDDLE)
     for q, span in enumerate(quarters):
-        forward, mirror = sums(q, 256, 512, MID, LATE)
-        zf[span, :] += forward
-        zm[span, :] += mirror
+        forward, mirror = sums(q, 0, 512, 0, LATE)
+        zf[span, :] = forward
+        zm[span, :] = mirror + mm(own_counts[span, :], own_twice)
 
     wait_for(CORNERS)
     save = pltpu.make_async_copy(blocks, blocks_hbm, in_sem.at[4])

time: 39.3 us -> 39.3 us (level)
  the two profiles are of different devices: /device:TPU:43 before, /device:TPU:41 now
where the time goes in v5:
time: 39.3 us; the launch traced here: 39.1 us
  Pallas kernels  38.5 us (98%)
  between operations  0.66 us (2%)
    pallas_call x1, Pallas kernels, local(): pl.pallas_call(functools.partial(main_kernel, nx, ny, nz), out_shape=[jax...  36.8 us
    pallas_call x1, Pallas kernels, local(): pl.pallas_call(remainder_kernel, out_shape=jax.ShapeDtypeStruct((BOXES, P...  1.67 us

profile of v5, /device:TPU:41, one launch (start us, length us, event | category | flops | bytes accessed | tf_op | source)
XLA Modules:
  0.0 39.1 jit_solution(14451054141436027025)
XLA Ops:
  0.7 36.8 %exchange.1 = (f32[72,256]{1,0:T(8,128)}, bf16[27,80,256]{2,1,0:T(8,128)(2,1)}) custom-call(s32[1]{0:T(128)S(6)} %copy.6.count_ref, s32[3,1024]{1,0:T(4,128)} %pairs_hbm.1, s32[624]{0:T(1024)} %send_hbm.1, bf16[64,256]{1,0:T(8,128)(2,1)} %m_hbm.1, bf16[16,256,256]{2,1,0:T(8,128)(2,1)} %ops_hbm.3), custom_call_target="tpu_custom_call" | custom-call | tf_op jit(solution)/shard_map/exchange/pallas_call | solution.py:503
  37.5 1.7 %remainder.1 = f32[64,256]{1,0:T(8,128)} custom-call(f32[72,256]{1,0:T(8,128)} %get-tuple-element.7.field_hbm, bf16[27,80,256]{2,1,0:T(8,128)(2,1)} %get-tuple-element.8.blocks_hbm, bf16[16,256,256]{2,1,0:T(8,128)(2,1)} %ops_hbm.3), custom_call_target="tpu_custom_call" | custom-call | tf_op jit(solution)/shard_map/remainder/pallas_call | solution.py:538

commit v6 on v5

--- a/solution.py
+++ b/solution.py
@@ -466,12 +466,12 @@
 
     ghost[0:BOXES, :] = blocks[OWN, 0:BOXES, :]
     starts_v[0:27, :] = jnp.zeros((27, 128), I32)
-    wait_for(EARLY)
-    take(EARLY)
     own = blocks[OWN, 0:BOXES, :]
     own_twice = jnp.concatenate([own, own], axis=0)
     quarters = [slice(256 * q, 256 * (q + 1)) for q in range(4)]
     relay(along_yz, "x", 0)
+    wait_for(EARLY)
+    take(EARLY)
     wait_for(MIDDLE)
     take(MIDDLE)
     for q, span in enumerate(quarters):

time: 39.3 us -> 39.5 us (level)
  the two profiles are of different devices: /device:TPU:41 before, /device:TPU:58 now
where the time goes in v6:
time: 39.5 us; the launch traced here: 39.3 us
  Pallas kernels  38.7 us (98%)
  between operations  0.66 us (2%)
    pallas_call x1, Pallas kernels, local(): pl.pallas_call(functools.partial(main_kernel, nx, ny, nz), out_shape=[jax...  37 us
    pallas_call x1, Pallas kernels, local(): pl.pallas_call(remainder_kernel, out_shape=jax.ShapeDtypeStruct((BOXES, P...  1.67 us

profile of v6, /device:TPU:58, one launch (start us, length us, event | category | flops | bytes accessed | tf_op | source)
XLA Modules:
  0.0 39.3 jit_solution(14940294474991925821)
XLA Ops:
  0.7 37.0 %exchange.1 = (f32[72,256]{1,0:T(8,128)}, bf16[27,80,256]{2,1,0:T(8,128)(2,1)}) custom-call(s32[1]{0:T(128)S(6)} %copy.6.count_ref, s32[3,1024]{1,0:T(4,128)} %pairs_hbm.1, s32[624]{0:T(1024)} %send_hbm.1, bf16[64,256]{1,0:T(8,128)(2,1)} %m_hbm.1, bf16[16,256,256]{2,1,0:T(8,128)(2,1)} %ops_hbm.3), custom_call_target="tpu_custom_call" | custom-call | tf_op jit(solution)/shard_map/exchange/pallas_call | solution.py:503
  37.7 1.7 %remainder.1 = f32[64,256]{1,0:T(8,128)} custom-call(f32[72,256]{1,0:T(8,128)} %get-tuple-element.7.field_hbm, bf16[27,80,256]{2,1,0:T(8,128)(2,1)} %get-tuple-element.8.blocks_hbm, bf16[16,256,256]{2,1,0:T(8,128)(2,1)} %ops_hbm.3), custom_call_target="tpu_custom_call" | custom-call | tf_op jit(solution)/shard_map/remainder/pallas_call | solution.py:538

commit v7 on v4

--- a/solution.py
+++ b/solution.py
@@ -441,8 +441,8 @@
     )
     count_own(count, pairs_ref, own_counts, hot_t)
     count_forward(count, pairs_ref, counts, hot_u)
+    relay(along_z, "yx", 0)
     relay(along_y, "x", 0)
-    relay(along_z, "yx", 0)
     loads[3].wait()
 
     def take(lanes):

time: 39.3 us -> 39.4 us (level)
  no operation moved by 1% of the time
where the time goes in v7:
time: 39.4 us; the launch traced here: 39.2 us
  Pallas kernels  38.6 us (98%)
  between operations  0.66 us (2%)
    pallas_call x1, Pallas kernels, local(): pl.pallas_call(functools.partial(main_kernel, nx, ny, nz), out_shape=[jax...  36.9 us
    pallas_call x1, Pallas kernels, local(): pl.pallas_call(remainder_kernel, out_shape=jax.ShapeDtypeStruct((BOXES, P...  1.67 us

profile of v7, /device:TPU:43, one launch (start us, length us, event | category | flops | bytes accessed | tf_op | source)
XLA Modules:
  0.0 39.2 jit_solution(8301059136786293573)
XLA Ops:
  0.7 36.9 %exchange.1 = (f32[72,256]{1,0:T(8,128)}, bf16[27,80,256]{2,1,0:T(8,128)(2,1)}) custom-call(s32[1]{0:T(128)S(6)} %copy.6.count_ref, s32[3,1024]{1,0:T(4,128)} %pairs_hbm.1, s32[624]{0:T(1024)} %send_hbm.1, bf16[64,256]{1,0:T(8,128)(2,1)} %m_hbm.1, bf16[16,256,256]{2,1,0:T(8,128)(2,1)} %ops_hbm.3), custom_call_target="tpu_custom_call" | custom-call | tf_op jit(solution)/shard_map/exchange/pallas_call | solution.py:508
  37.5 1.7 %remainder.1 = f32[64,256]{1,0:T(8,128)} custom-call(f32[72,256]{1,0:T(8,128)} %get-tuple-element.7.field_hbm, bf16[27,80,256]{2,1,0:T(8,128)(2,1)} %get-tuple-element.8.blocks_hbm, bf16[16,256,256]{2,1,0:T(8,128)(2,1)} %ops_hbm.3), custom_call_target="tpu_custom_call" | custom-call | tf_op jit(solution)/shard_map/remainder/pallas_call | solution.py:543
